TPU v7x, 128 devices: a whole 4x4x4 slice. The times are simulated.
128 devices in a mesh: pin: 32 (over z, x, core), board: 4 (over y).
Axes of the slice: x: 4, y: 4, z: 4, core: 2. Of those that a mesh axis runs over, the one named last changes fastest.
Arguments:
- features: bfloat16 [65536, 2048], P(('pin', 'board')), may hold values from -6 to 6
- w_message: bfloat16 [2048, 1024], replicated, may hold values from -0.125 to 0.125
- w_update: bfloat16 [1024, 1024], replicated, may hold values from -0.375 to 0.375
- cotangent: bfloat16 [65536, 1024], P(('pin', 'board')), may hold values from -6 to 6
- slot_pin: int32 [128, 128, 16], P(('pin', 'board')), may hold values from 0 to 511
- slot_board: int32 [128, 128, 16], P(('pin', 'board')), may hold values from 0 to 255
- slot_walk: int32 [128, 128, 16], P(('pin', 'board')), may hold values from 1 to 32, as said below
- pair_count: int32 [128, 128], P(('pin', 'board')), may hold values from 1 to 16, as said below
Outputs:
- output: bfloat16 [65536, 1024], P(('pin', 'board'))
- grad_message: bfloat16 [2048, 1024], replicated
- grad_update: bfloat16 [1024, 1024], replicated
Inputs may be any that keep to these rules, and one draw needn't show every extreme that they name: `slot_walk`: slots at or past their block's count hold arbitrary values in range. `pair_count`: in every draw some device receives 16 live slots from every device.
All inputs are finite; a program needn't handle non-finite values.
Results may differ from a plain program's by a relative error of at most 0.006.
The roundings to bfloat16 on the way count: a program that leaves them out, or rounds other values in their place, can miss the bound.
Values may be sent and summed in bfloat16 or wider, within the bound.
A program may use at most 128 MiB of HBM per device.

v0:
```python
import jax
import jax.numpy as jnp
from jax import lax
from jax.sharding import PartitionSpec as P


def silu_slope(value):
    sig = jax.nn.sigmoid(value)
    return sig * (1.0 + value * (1.0 - sig))


def body(features, w_message, w_update, cotangent, slot_pin, slot_board, slot_walk, pair_count):
    pin_count = lax.axis_size("pin")
    board_count = lax.axis_size("board")
    devices_all = pin_count * board_count
    slots = slot_pin.shape[2]
    pin_rows = features.shape[0]
    board_rows_dev = pin_rows // 2
    width = w_message.shape[1]
    slot_index = jnp.arange(slots, dtype=jnp.int32)
    is_live = slot_index[None, :] < pair_count[0][:, None]
    walks_int = jnp.where(is_live, slot_walk[0], 0)
    walks_flat = walks_int.reshape(-1).astype(jnp.float32)
    pins_flat = slot_pin[0].reshape(-1)
    pre_act = jnp.dot(features, w_message, preferred_element_type=jnp.float32)
    hidden = jax.nn.silu(pre_act).astype(jnp.bfloat16)
    messages = jnp.take(hidden, pins_flat, axis=0).reshape(devices_all, slots, width)
    boards_sent = slot_board[0]
    recv_messages, recv_boards, recv_walks = (
        lax.all_to_all(messages, ("pin", "board"), split_axis=0, concat_axis=0, tiled=True),
        lax.all_to_all(boards_sent, ("pin", "board"), split_axis=0, concat_axis=0, tiled=True),
        lax.all_to_all(walks_int, ("pin", "board"), split_axis=0, concat_axis=0, tiled=True),
    )
    recv_board_flat = recv_boards.reshape(-1)
    recv_weight = recv_walks.reshape(-1).astype(jnp.float32)
    board_match = jnp.arange(board_rows_dev, dtype=jnp.int32)[:, None] == recv_board_flat[None, :]
    board_weights = jnp.where(board_match, recv_weight[None, :], 0.0)
    board_degree = jnp.sum(board_weights, axis=1)
    board_total = jnp.dot(
        board_weights.astype(jnp.bfloat16),
        recv_messages.reshape(-1, width),
        preferred_element_type=jnp.float32,
    )
    board_rows = (board_total / jnp.maximum(board_degree, 1.0)[:, None]).astype(jnp.bfloat16)
    returned = jnp.take(board_rows, recv_board_flat, axis=0).reshape(devices_all, slots, width)
    read_rows = lax.all_to_all(returned, ("pin", "board"), split_axis=0, concat_axis=0, tiled=True)
    pin_match = jnp.arange(pin_rows, dtype=jnp.int32)[:, None] == pins_flat[None, :]
    pin_weights = jnp.where(pin_match, walks_flat[None, :], 0.0)
    pin_degree = jnp.sum(pin_weights, axis=1)
    neigh_total = jnp.dot(
        pin_weights.astype(jnp.bfloat16),
        read_rows.reshape(-1, width),
        preferred_element_type=jnp.float32,
    )
    neighbour = (neigh_total / jnp.maximum(pin_degree, 1.0)[:, None]).astype(jnp.bfloat16)
    update = jnp.dot(neighbour, w_update, preferred_element_type=jnp.float32)
    output = (hidden.astype(jnp.float32) + jax.nn.silu(update)).astype(jnp.bfloat16)
    d_update = (cotangent.astype(jnp.float32) * silu_slope(update)).astype(jnp.bfloat16)
    grad_update = lax.dot_general(
        neighbour, d_update, (((0,), (0,)), ((), ())), preferred_element_type=jnp.float32
    )
    d_neighbour = lax.dot_general(
        d_update, w_update, (((1,), (1,)), ((), ())), preferred_element_type=jnp.float32
    ).astype(jnp.bfloat16)
    slot_scale = walks_flat / jnp.maximum(jnp.take(pin_degree, pins_flat, axis=0), 1.0)
    slot_grad = (
        slot_scale[:, None] * jnp.take(d_neighbour, pins_flat, axis=0).astype(jnp.float32)
    ).astype(jnp.bfloat16)
    slot_grad = slot_grad.reshape(devices_all, slots, width)
    recv_grads = lax.all_to_all(
        slot_grad, ("pin", "board"), split_axis=0, concat_axis=0, tiled=True
    )
    board_sum = jnp.dot(
        board_match.astype(jnp.bfloat16),
        recv_grads.reshape(-1, width),
        preferred_element_type=jnp.float32,
    )
    board_grad = board_sum / jnp.maximum(board_degree, 1.0)[:, None]
    message_grad = (recv_weight[:, None] * jnp.take(board_grad, recv_board_flat, axis=0)).astype(
        jnp.bfloat16
    )
    message_grad = message_grad.reshape(devices_all, slots, width)
    back_grads = lax.all_to_all(
        message_grad, ("pin", "board"), split_axis=0, concat_axis=0, tiled=True
    )
    neigh_grad = jnp.dot(
        pin_match.astype(jnp.bfloat16),
        back_grads.reshape(-1, width),
        preferred_element_type=jnp.float32,
    )
    hidden_grad = cotangent.astype(jnp.float32) + neigh_grad
    d_pre = (hidden_grad * silu_slope(pre_act)).astype(jnp.bfloat16)
    grad_message = lax.dot_general(
        features, d_pre, (((0,), (0,)), ((), ())), preferred_element_type=jnp.float32
    )
    total_message, total_update = lax.psum((grad_message, grad_update), ("pin", "board"))
    return (output, total_message.astype(jnp.bfloat16), total_update.astype(jnp.bfloat16))


def solution(mesh):
    in_specs = (
        P(("pin", "board"), None),
        P(),
        P(),
        P(("pin", "board"), None),
        P(("pin", "board"), None, None),
        P(("pin", "board"), None, None),
        P(("pin", "board"), None, None),
        P(("pin", "board"), None),
    )
    out_specs = (P(("pin", "board"), None), P(), P())
    return jax.shard_map(body, mesh=mesh, in_specs=in_specs, out_specs=out_specs, check_vma=False)
```

profile of v0, /device:TPU:1, one launch (start us, length us, event | category | flops | bytes accessed | tf_op | source)
XLA Modules:
  0.0 491.1 jit_solution(6893740091082586250)
XLA Ops:
  0.6 0.0 copy-start
  0.6 0.9 copy.30
  1.6 1.5 compare_select_fusion
  3.1 11.5 %all-to-all-start.1 = ((s32[128,1,16]{2,1,0:T(1,128)}), s32[128,1,16]{2,1,0:T(1,128)S(1)}, u32[]{:S(2)}, u32[]{:S(2)}) async-start(s32[128,1,16]{2,1,0:T(1,128)} %compare_select_fusion), calls=%async_computation.1 | async-start | bytes 131072 | tf_op jit(solution)/shard_map/all_to_all | solution.py:32
  14.6 0.7 iota_compare_fusion.10
  15.3 0.8 copy.29
  16.1 0.1 eq.29
  16.2 0.1 reshape_squeeze.3
  16.3 0.1 squeeze.6
  16.4 0.1 lt.96
  16.5 0.5 select_reduce_fusion
  17.0 13.2 %gather_fusion.1 = f32[2048]{0:T(1024)S(1)} fusion(f32[512]{0:T(512)S(1)} %select_reduce_fusion, s32[2048]{0:T(1024)S(1)} %broadcast_clamp_fusion.1), kind=kCustom, calls=%fused_computation.3 | custom fusion | bytes 24576 | tf_op jit(solution)/shard_map/jit(_take)/gather | solution.py:65
  30.3 0.0 copy-done
  30.3 0.0 copy-start.6
  30.3 6.0 %multiply_convert_fusion.2 = (bf16[512,1024]{1,0:T(8,128)(2,1)S(1)}, f32[512,1024]{1,0:T(8,128)}) fusion(bf16[512,2048]{1,0:T(8,128)(2,1)S(1)} %copy-done, bf16[2048,1024]{1,0:T(8,128)(2,1)} %param.11), kind=kOutput, calls=%fused_computation.31 | convolution fusion | flops 2150105088 | bytes 9437184 | tf_op jit(solution)/shard_map/dot_general | solution.py:25
  36.3 0.0 copy-start.1
  36.3 0.0 copy-done.6
  36.3 0.8 copy.31
  37.1 9.6 %gather_fusion.3 = bf16[2048,1024]{1,0:T(8,128)(2,1)} fusion(bf16[512,1024]{1,0:T(8,128)(2,1)S(1)} %get-tuple-element.22, s32[2048]{0:T(1024)S(1)} %fusion.16), kind=kCustom, calls=%fused_computation.clone | custom fusion | bytes 8396800 | tf_op jit(solution)/shard_map/jit(_take)/gather | solution.py:27
  46.8 0.0 copy-done.1
  46.8 0.0 all-to-all-done.1
  46.8 9.8 %all-to-all-start = ((s32[128,1,16]{2,1,0:T(1,128)}), s32[128,1,16]{2,1,0:T(1,128)S(1)}, u32[]{:S(2)}, u32[]{:S(2)}) async-start(s32[128,1,16]{2,1,0:T(1,128)} %bitcast.1), calls=%async_computation | async-start | bytes 131072 | tf_op jit(solution)/shard_map/all_to_all | solution.py:31
  56.5 3.9 broadcast_select_fusion
  60.4 5.8 %all-to-all-done = s32[128,1,16]{2,1,0:T(1,128)S(1)} async-done(((s32[128,1,16]{2,1,0:T(1,128)}), s32[128,1,16]{2,1,0:T(1,128)S(1)}, u32[]{:S(2)}, u32[]{:S(2)}) %all-to-all-start) | async-done | bytes 8224 | tf_op jit(solution)/shard_map/all_to_all | solution.py:31
  66.2 5.3 %all-to-all-start.2 = ((bf16[128,16,1024]{2,1,0:T(8,128)(2,1)}), bf16[128,16,1024]{2,1,0:T(8,128)(2,1)}, u32[]{:S(2)}, u32[]{:S(2)}) async-start(bf16[128,16,1024]{2,1,0:T(8,128)(2,1)} %bitcast.33), calls=%async_computation.2 | async-start | bytes 8388608 | tf_op jit(solution)/shard_map/all_to_all | solution.py:30
  71.5 0.2 convert_reduce_fusion
  71.6 0.1 convert_element_type.85
  71.7 0.1 reshape.255
  71.8 0.6 broadcast.161
  72.4 0.8 reduce.9
  73.2 0.1 reshape.252
  73.3 0.3 select_reduce_fusion.1
  73.7 50.8 %all-to-all-done.2 = bf16[128,16,1024]{2,1,0:T(8,128)(2,1)} async-done(((bf16[128,16,1024]{2,1,0:T(8,128)(2,1)}), bf16[128,16,1024]{2,1,0:T(8,128)(2,1)}, u32[]{:S(2)}, u32[]{:S(2)}) %all-to-all-start.2) | async-done | bytes 4194336 | tf_op jit(solution)/shard_map/all_to_all | solution.py:30
  124.4 3.4 fusion.10
  127.9 9.6 %gather_fusion = bf16[2048,1024]{1,0:T(8,128)(2,1)} fusion(bf16[256,1024]{1,0:T(8,128)(2,1)S(1)} %fusion.10, s32[2048]{0:T(1024)S(1)} %broadcast_clamp_fusion), kind=kCustom, calls=%fused_computation.2 | custom fusion | bytes 8396800 | tf_op jit(solution)/shard_map/jit(_take)/gather | solution.py:45
  137.5 3.9 broadcast_select_fusion.1
  141.4 5.0 %all-to-all-start.3 = ((bf16[128,16,1024]{2,1,0:T(8,128)(2,1)}), bf16[128,16,1024]{2,1,0:T(8,128)(2,1)}, u32[]{:S(2)}, u32[]{:S(2)}) async-start(bf16[128,16,1024]{2,1,0:T(8,128)(2,1)} %broadcast_select_fusion.1), calls=%async_computation.3 | async-start | bytes 8388608 | tf_op jit(solution)/shard_map/all_to_all | solution.py:46
  146.3 52.4 %all-to-all-done.3 = bf16[128,16,1024]{2,1,0:T(8,128)(2,1)} async-done(((bf16[128,16,1024]{2,1,0:T(8,128)(2,1)}), bf16[128,16,1024]{2,1,0:T(8,128)(2,1)}, u32[]{:S(2)}, u32[]{:S(2)}) %all-to-all-start.3) | async-done | bytes 4194336 | tf_op jit(solution)/shard_map/all_to_all | solution.py:46
  198.7 0.0 copy-start.2
  198.7 0.0 copy-start.7
  198.7 0.0 copy-start.8
  198.7 4.7 divide_convert_fusion
  203.4 0.0 copy-done.2
  203.4 0.0 copy-done.7
  203.4 0.0 copy-done.8
  203.4 0.0 copy-start.3
  203.4 3.1 fusion.1
  206.5 0.0 copy-done.3
  206.5 1.0 copy-done.5
  207.5 1.3 convolution_convert_fusion
  208.8 9.6 %gather_fusion.4 = bf16[2048,1024]{1,0:T(8,128)(2,1)} fusion(bf16[512,1024]{1,0:T(8,128)(2,1)S(1)} %convolution_convert_fusion, s32[2048]{0:T(1024)S(1)} %fusion.16), kind=kCustom, calls=%fused_computation.1.clone | custom fusion | bytes 8396800 | tf_op jit(solution)/shard_map/jit(_take)/gather | solution.py:67
  218.4 4.2 multiply_convert_fusion.1
  222.6 4.8 all-to-all-start.4
  227.4 52.5 %all-to-all-done.4 = bf16[128,16,1024]{2,1,0:T(8,128)(2,1)} async-done(((bf16[128,16,1024]{2,1,0:T(8,128)(2,1)}), bf16[128,16,1024]{2,1,0:T(8,128)(2,1)}, u32[]{:S(2)}, u32[]{:S(2)}) %all-to-all-start.4) | async-done | bytes 4194336 | tf_op jit(solution)/shard_map/all_to_all | solution.py:70
  280.0 3.4 fusion.11
  283.4 9.9 %gather_fusion.2 = f32[2048,1024]{1,0:T(8,128)} fusion(f32[256,1024]{1,0:T(8,128)S(1)} %fusion.11, s32[2048]{0:T(1024)S(1)} %broadcast_clamp_fusion), kind=kCustom, calls=%fused_computation.4 | custom fusion | bytes 16785408 | tf_op jit(solution)/shard_map/jit(_take)/gather | solution.py:79
  293.3 5.3 %multiply_convert_fusion = bf16[128,16,1024]{2,1,0:T(8,128)(2,1)} fusion(f32[128,16,1024]{2,1,0:T(8,128)} %bitcast.31, f32[128,16]{1,0:T(8,128)S(1)} %bitcast.38, pred[128,16]{1,0:T(8,128)(4,1)S(1)} %compare_and_fusion), kind=kLoop, calls=%fused_computation.5 | loop fusion | flops 6291456 | bytes 12593152 | tf_op jit(solution)/shard_map/convert_element_type | solution.py:79
  298.6 5.1 %all-to-all-start.5 = ((bf16[128,16,1024]{2,1,0:T(8,128)(2,1)}), bf16[128,16,1024]{2,1,0:T(8,128)(2,1)}, u32[]{:S(2)}, u32[]{:S(2)}) async-start(bf16[128,16,1024]{2,1,0:T(8,128)(2,1)} %multiply_convert_fusion), calls=%async_computation.5 | async-start | bytes 8388608 | tf_op jit(solution)/shard_map/all_to_all | solution.py:83
  303.7 0.0 copy-done.4
  303.7 4.4 fusion.20
  308.1 47.9 %all-to-all-done.5 = bf16[128,16,1024]{2,1,0:T(8,128)(2,1)} async-done(((bf16[128,16,1024]{2,1,0:T(8,128)(2,1)}), bf16[128,16,1024]{2,1,0:T(8,128)(2,1)}, u32[]{:S(2)}, u32[]{:S(2)}) %all-to-all-start.5) | async-done | bytes 4194336 | tf_op jit(solution)/shard_map/all_to_all | solution.py:83
  356.0 11.1 %convolution_bitcast_fusion = f32[2048,1024]{0,1:T(8,128)} fusion(bf16[512,2048]{1,0:T(8,128)(2,1)S(1)} %copy-done, bf16[512,1024]{1,0:T(8,128)(2,1)} %param.13, f32[512,1024]{1,0:T(8,128)} %get-tuple-element.23, bf16[2048,1024]{1,0:T(8,128)(2,1)} %bitcast.14, s32[2048]{0:T(1024)S(1)} %eq.29), kind=kOutput, calls=%fused_computation.9 | convolution fusion | flops 4301783040 | bytes 17833984 | tf_op jit(solution)/shard_map/dot_general | solution.py:93
  367.2 117.5 %all-reduce.2 = (bf16[2048,1024]{0,1:T(8,128)(2,1)}, bf16[1024,1024]{1,0:T(8,128)(2,1)}) all-reduce(f32[2048,1024]{0,1:T(8,128)} %convolution_bitcast_fusion, f32[1024,1024]{1,0:T(8,128)} %fusion.20), channel_id=1, replica_groups=mesh['pin'=32,'board'=4] {'pin','board'}, use_global_device_ids=true, to_apply=%region_2.4 | all-reduce | flops 3145728 | bytes 18874368 | tf_op jit(solution)/shard_map/psum | solution.py:96
  484.7 6.4 %copy.34 = bf16[2048,1024]{1,0:T(8,128)(2,1)} copy(bf16[2048,1024]{0,1:T(8,128)(2,1)} %get-tuple-element.16) | data formatting | bytes 8388608
  (13 shorter events, 0.1 us)
Async XLA Ops:
  0.6 29.6 %copy-start = (bf16[512,2048]{1,0:T(8,128)(2,1)S(1)}, bf16[512,2048]{1,0:T(8,128)(2,1)}, u32[]{:S(2)}) copy-start(bf16[512,2048]{1,0:T(8,128)(2,1)} %param.10) | copy-start | bytes 6291460
  3.1 43.7 %all-to-all-start.1 = ((s32[128,1,16]{2,1,0:T(1,128)}), s32[128,1,16]{2,1,0:T(1,128)S(1)}, u32[]{:S(2)}, u32[]{:S(2)}) async-start(s32[128,1,16]{2,1,0:T(1,128)} %compare_select_fusion), calls=%async_computation.1 | async-start | bytes 131072 | tf_op jit(solution)/shard_map/all_to_all | solution.py:32
  30.3 6.0 %copy-start.6 = (s32[1,128,16]{1,2,0:T(8,128)S(1)}, s32[1,128,16]{1,2,0:T(8,128)}, u32[]{:S(2)}) copy-start(s32[1,128,16]{1,2,0:T(8,128)} %param.15) | copy-start | bytes 24580
  36.3 10.5 %copy-start.1 = (bf16[512,1024]{1,0:T(8,128)(2,1)}, bf16[512,1024]{1,0:T(8,128)(2,1)S(1)}, u32[]{:S(2)}) copy-start(bf16[512,1024]{1,0:T(8,128)(2,1)S(1)} %get-tuple-element.22) | copy-start | bytes 3145732
  46.8 19.4 %all-to-all-start = ((s32[128,1,16]{2,1,0:T(1,128)}), s32[128,1,16]{2,1,0:T(1,128)S(1)}, u32[]{:S(2)}, u32[]{:S(2)}) async-start(s32[128,1,16]{2,1,0:T(1,128)} %bitcast.1), calls=%async_computation | async-start | bytes 131072 | tf_op jit(solution)/shard_map/all_to_all | solution.py:31
  66.2 58.3 %all-to-all-start.2 = ((bf16[128,16,1024]{2,1,0:T(8,128)(2,1)}), bf16[128,16,1024]{2,1,0:T(8,128)(2,1)}, u32[]{:S(2)}, u32[]{:S(2)}) async-start(bf16[128,16,1024]{2,1,0:T(8,128)(2,1)} %bitcast.33), calls=%async_computation.2 | async-start | bytes 8388608 | tf_op jit(solution)/shard_map/all_to_all | solution.py:30
  141.4 57.4 %all-to-all-start.3 = ((bf16[128,16,1024]{2,1,0:T(8,128)(2,1)}), bf16[128,16,1024]{2,1,0:T(8,128)(2,1)}, u32[]{:S(2)}, u32[]{:S(2)}) async-start(bf16[128,16,1024]{2,1,0:T(8,128)(2,1)} %broadcast_select_fusion.1), calls=%async_computation.3 | async-start | bytes 8388608 | tf_op jit(solution)/shard_map/all_to_all | solution.py:46
  198.7 4.7 copy-start.2
  198.7 4.7 copy-start.7
  198.7 4.7 copy-start.8
  203.4 3.1 copy-start.3
  206.5 1.0 copy-start.5
  222.6 57.4 %all-to-all-start.4 = ((bf16[128,16,1024]{2,1,0:T(8,128)(2,1)}), bf16[128,16,1024]{2,1,0:T(8,128)(2,1)}, u32[]{:S(2)}, u32[]{:S(2)}) async-start(bf16[128,16,1024]{2,1,0:T(8,128)(2,1)} %bitcast.34), calls=%async_computation.4 | async-start | bytes 8388608 | tf_op jit(solution)/shard_map/all_to_all | solution.py:70
  298.6 5.1 %copy-start.4 = (bf16[512,1024]{1,0:T(8,128)(2,1)S(1)}, bf16[512,1024]{1,0:T(8,128)(2,1)}, u32[]{:S(2)}) copy-start(bf16[512,1024]{1,0:T(8,128)(2,1)} %copy-done.3) | copy-start | bytes 3145732
  298.6 57.5 %all-to-all-start.5 = ((bf16[128,16,1024]{2,1,0:T(8,128)(2,1)}), bf16[128,16,1024]{2,1,0:T(8,128)(2,1)}, u32[]{:S(2)}, u32[]{:S(2)}) async-start(bf16[128,16,1024]{2,1,0:T(8,128)(2,1)} %multiply_convert_fusion), calls=%async_computation.5 | async-start | bytes 8388608 | tf_op jit(solution)/shard_map/all_to_all | solution.py:83
where the time goes:
time: 492 us; the launch traced here: 491 us
  waiting for transfers between devices  209 us (42%)
  blocking collectives  118 us (24%)
  local copies, waits for them, and re-layouts  63.1 us (13%)
  starting transfers between devices  41.4 us (8%)
  matrix products  37.5 us (8%)
  other arithmetic  21.3 us (4%)
    psum x1, blocking collectives, body(): lax.psum((grad_message, grad_update), ('pin', 'board'))  118 us
    all_to_all x1, waiting for transfers between devices, body(): lax.all_to_all(slot_grad, ('pin', 'board'), split_axis=0, concat_axis=0,...  52.5 us
    all_to_all x1, waiting for transfers between devices, body(): lax.all_to_all(returned, ('pin', 'board'), split_axis=0, concat_axis=0, t...  52.4 us
    all_to_all x1, waiting for transfers between devices, body(): lax.all_to_all(messages, ('pin', 'board'), split_axis=0, concat_axis=0, t...  50.8 us
    all_to_all x1, waiting for transfers between devices, body(): lax.all_to_all(message_grad, ('pin', 'board'), split_axis=0, concat_axis=...  47.9 us
    gather x1, local copies, waits for them, and re-layouts, body(): jnp.take(pin_degree, pins_flat, axis=0)  13.2 us
    all_to_all x1, starting transfers between devices, body(): lax.all_to_all(walks_int, ('pin', 'board'), split_axis=0, concat_axis=0,...  11.5 us
    dot_general x1, matrix products, body(): lax.dot_general(features, d_pre, (((0,), (0,)), ((), ())), preferred_elem...  11.1 us
  transfers between devices with their start and end apart: 6, of which 5 were waited for; matrix products, arithmetic and copies ran while one was open for 9% of the time, Pallas kernels for 0%

commit v1 on v0

--- a/solution.py
+++ b/solution.py
@@ -1,7 +1,61 @@
 import jax
 import jax.numpy as jnp
 from jax import lax
+from jax.experimental import pallas as pl
+from jax.experimental.pallas import tpu as pltpu
 from jax.sharding import PartitionSpec as P
+
+MESH = pl.DeviceIdType.MESH
+
+
+def peer_of(step):
+    pin = lax.axis_index("pin")
+    board = lax.axis_index("board")
+    dz, dx, dc, dy = step // 32, (step // 8) % 4, (step // 4) % 2, step % 4
+    z, x, c = pin // 8, (pin // 2) % 4, pin % 2
+    peer_pin = ((z + dz) % 4) * 8 + ((x + dx) % 4) * 2 + (c + dc) % 2
+    return peer_pin, (board + dy) % 4
+
+
+def exchange_kernel(x_ref, o_ref, send_sem, recv_sem, own_sem):
+    me = lax.axis_index("pin") * 4 + lax.axis_index("board")
+    barrier = pltpu.get_barrier_semaphore()
+
+    @pl.loop(1, 128)
+    def _(step):
+        pl.semaphore_signal(barrier, inc=1, device_id=peer_of(step), device_id_type=MESH)
+
+    pl.semaphore_wait(barrier, 127)
+    own = pltpu.make_async_copy(x_ref.at[me], o_ref.at[me], own_sem)
+    own.start()
+
+    @pl.loop(1, 128)
+    def _(step):
+        pin, board = peer_of(step)
+        pltpu.make_async_remote_copy(
+            x_ref.at[pin * 4 + board],
+            o_ref.at[me],
+            send_sem,
+            recv_sem,
+            device_id=(pin, board),
+            device_id_type=MESH,
+        ).start()
+
+    own.wait()
+    part = pl.ds(0, 127)
+    pltpu.make_async_copy(x_ref.at[part], x_ref.at[part], send_sem).wait()
+    pltpu.make_async_copy(o_ref.at[part], o_ref.at[part], recv_sem).wait()
+
+
+def exchange(x):
+    return pl.pallas_call(
+        exchange_kernel,
+        out_shape=jax.ShapeDtypeStruct(x.shape, x.dtype),
+        in_specs=[pl.BlockSpec(memory_space=pl.ANY)],
+        out_specs=pl.BlockSpec(memory_space=pl.ANY),
+        scratch_shapes=[pltpu.SemaphoreType.DMA] * 3,
+        compiler_params=pltpu.CompilerParams(collective_id=0, has_side_effects=True),
+    )(x)
 
 
 def silu_slope(value):
@@ -27,7 +81,7 @@
     messages = jnp.take(hidden, pins_flat, axis=0).reshape(devices_all, slots, width)
     boards_sent = slot_board[0]
     recv_messages, recv_boards, recv_walks = (
-        lax.all_to_all(messages, ("pin", "board"), split_axis=0, concat_axis=0, tiled=True),
+        exchange(messages),
         lax.all_to_all(boards_sent, ("pin", "board"), split_axis=0, concat_axis=0, tiled=True),
         lax.all_to_all(walks_int, ("pin", "board"), split_axis=0, concat_axis=0, tiled=True),
     )
@@ -43,7 +97,7 @@
     )
     board_rows = (board_total / jnp.maximum(board_degree, 1.0)[:, None]).astype(jnp.bfloat16)
     returned = jnp.take(board_rows, recv_board_flat, axis=0).reshape(devices_all, slots, width)
-    read_rows = lax.all_to_all(returned, ("pin", "board"), split_axis=0, concat_axis=0, tiled=True)
+    read_rows = exchange(returned)
     pin_match = jnp.arange(pin_rows, dtype=jnp.int32)[:, None] == pins_flat[None, :]
     pin_weights = jnp.where(pin_match, walks_flat[None, :], 0.0)
     pin_degree = jnp.sum(pin_weights, axis=1)
@@ -67,9 +121,7 @@
         slot_scale[:, None] * jnp.take(d_neighbour, pins_flat, axis=0).astype(jnp.float32)
     ).astype(jnp.bfloat16)
     slot_grad = slot_grad.reshape(devices_all, slots, width)
-    recv_grads = lax.all_to_all(
-        slot_grad, ("pin", "board"), split_axis=0, concat_axis=0, tiled=True
-    )
+    recv_grads = exchange(slot_grad)
     board_sum = jnp.dot(
         board_match.astype(jnp.bfloat16),
         recv_grads.reshape(-1, width),
@@ -80,9 +132,7 @@
         jnp.bfloat16
     )
     message_grad = message_grad.reshape(devices_all, slots, width)
-    back_grads = lax.all_to_all(
-        message_grad, ("pin", "board"), split_axis=0, concat_axis=0, tiled=True
-    )
+    back_grads = exchange(message_grad)
     neigh_grad = jnp.dot(
         pin_match.astype(jnp.bfloat16),
         back_grads.reshape(-1, width),

time: 492 us -> 597 us (1.21)
  Pallas kernels: 0 us -> 329 us
  waiting for transfers between devices: 209 us -> 9.66 us
  starting transfers between devices: 41.4 us -> 15.3 us
    pallas_call x0 -> x4, Pallas kernels: none -> 329 us  [exchange(): pl.pallas_call(exchange_kernel, out_shape=jax.ShapeDtypeStruct(x.shape, x...]
    all_to_all x4 -> x0, waiting for transfers between devices: 204 us -> none  [the longest x1 52.5 us: body(): lax.all_to_all(slot_grad, ('pin', 'board'), split_axis=0, concat_axis=0,...]
    all_to_all x4 -> x0, starting transfers between devices: 20.1 us -> none  [the longest x1 5.28 us: body(): lax.all_to_all(messages, ('pin', 'board'), split_axis=0, concat_axis=0, t...]
    all_to_all x1, waiting for transfers between devices: 0.01 us -> 9.65 us  [body(): lax.all_to_all(walks_int, ('pin', 'board'), split_axis=0, concat_axis=0,...]
    all_to_all x1, starting transfers between devices: 11.5 us -> 3.78 us  [body(): lax.all_to_all(walks_int, ('pin', 'board'), split_axis=0, concat_axis=0,...]
  transfers between devices with their start and end apart: 6 -> 2, of which waited for: 5 -> 1; matrix products, arithmetic and copies ran while one was open for 9% -> 6% of each run, Pallas kernels for 0% -> 15%
where the time goes in v1:
time: 597 us
  Pallas kernels  329 us (55%)
  blocking collectives  123 us (21%)
  local copies, waits for them, and re-layouts  62.5 us (10%)
  matrix products  36 us (6%)
  other arithmetic  20.7 us (3%)
  starting transfers between devices  15.3 us (3%)
  waiting for transfers between devices  9.66 us (2%)
    pallas_call x4, Pallas kernels, exchange(): pl.pallas_call(exchange_kernel, out_shape=jax.ShapeDtypeStruct(x.shape, x...  329 us
    psum x1, blocking collectives, body(): lax.psum((grad_message, grad_update), ('pin', 'board'))  123 us
    gather x1, local copies, waits for them, and re-layouts, body(): jnp.take(pin_degree, pins_flat, axis=0)  13.2 us
  transfers between devices with their start and end apart: 2, of which 1 were waited for; matrix products, arithmetic and copies ran while one was open for 6% of the time, Pallas kernels for 15%

profile of v1, /device:TPU:1, one launch (start us, length us, event | category | flops | bytes accessed | tf_op | source)
XLA Modules:
  0.0 596.8 jit_solution(2722052327742404462)
XLA Ops:
  0.6 0.0 copy-start
  0.6 1.6 copy.31
  2.2 11.5 %all-to-all-start = ((s32[128,1,16]{2,1,0:T(1,128)}), s32[128,1,16]{2,1,0:T(1,128)S(1)}, u32[]{:S(2)}, u32[]{:S(2)}) async-start(s32[128,1,16]{2,1,0:T(1,128)} %bitcast.1), calls=%async_computation | async-start | bytes 131072 | tf_op jit(solution)/shard_map/all_to_all | solution.py:85
  13.7 0.8 copy.29
  14.5 0.1 eq.29
  14.6 0.1 reshape_squeeze.3
  14.7 0.7 iota_compare_fusion.10
  15.4 0.1 lt.96
  15.6 0.8 copy.30
  16.4 0.1 squeeze.6
  16.5 0.5 select_reduce_fusion
  17.0 0.0 copy-start.3
  17.0 13.2 %gather_fusion.1 = f32[2048]{0:T(1024)S(1)} fusion(f32[512]{0:T(512)S(1)} %select_reduce_fusion, s32[2048]{0:T(1024)S(1)} %broadcast_clamp_fusion.1), kind=kCustom, calls=%fused_computation.3 | custom fusion | bytes 24576 | tf_op jit(solution)/shard_map/jit(_take)/gather | solution.py:119
  30.2 0.0 copy-done.3
  30.2 0.8 compare_select_fusion
  31.1 0.0 copy-done
  31.1 6.0 %multiply_convert_fusion.2 = (bf16[512,1024]{1,0:T(8,128)(2,1)S(1)}, f32[512,1024]{1,0:T(8,128)}) fusion(bf16[512,2048]{1,0:T(8,128)(2,1)S(1)} %copy-done, bf16[2048,1024]{1,0:T(8,128)(2,1)} %param.11), kind=kOutput, calls=%fused_computation.31 | convolution fusion | flops 2150105088 | bytes 9437184 | tf_op jit(solution)/shard_map/dot_general | solution.py:79
  37.1 0.0 copy-start.1
  37.1 9.6 %gather_fusion.3 = bf16[2048,1024]{1,0:T(8,128)(2,1)} fusion(bf16[512,1024]{1,0:T(8,128)(2,1)S(1)} %get-tuple-element.22, s32[2048]{0:T(1024)S(1)} %fusion.16), kind=kCustom, calls=%fused_computation.clone | custom fusion | bytes 8396800 | tf_op jit(solution)/shard_map/jit(_take)/gather | solution.py:81
  46.7 0.0 copy-done.1
  46.7 3.9 broadcast_select_fusion
  50.6 88.0 %shard_map.103 = bf16[128,16,1024]{2,1,0:T(8,128)(2,1)} custom-call(bf16[128,16,1024]{2,1,0:T(8,128)(2,1)} %bitcast.33), custom_call_target="tpu_custom_call" | custom-call | tf_op jit(solution)/shard_map/pallas_call | solution.py:51
  138.6 0.0 all-to-all-done
  138.6 3.8 all-to-all-start.1
  142.4 0.1 reshape.255
  142.5 9.7 %all-to-all-done.1 = s32[128,1,16]{2,1,0:T(1,128)S(1)} async-done(((s32[128,1,16]{2,1,0:T(1,128)}), s32[128,1,16]{2,1,0:T(1,128)S(1)}, u32[]{:S(2)}, u32[]{:S(2)}) %all-to-all-start.1) | async-done | bytes 8224 | tf_op jit(solution)/shard_map/all_to_all | solution.py:86
  152.2 0.2 convert_reduce_fusion
  152.3 0.1 convert_element_type.85
  152.4 0.5 broadcast.161
  153.0 0.8 reduce.9
  153.8 0.1 reshape.252
  153.9 0.3 select_reduce_fusion.1
  154.2 3.4 fusion.10
  157.6 9.6 %gather_fusion = bf16[2048,1024]{1,0:T(8,128)(2,1)} fusion(bf16[256,1024]{1,0:T(8,128)(2,1)S(1)} %fusion.10, s32[2048]{0:T(1024)S(1)} %broadcast_clamp_fusion), kind=kCustom, calls=%fused_computation.2 | custom fusion | bytes 8396800 | tf_op jit(solution)/shard_map/jit(_take)/gather | solution.py:99
  167.2 3.9 broadcast_select_fusion.1.x_ref
  171.1 77.7 %shard_map.104 = bf16[128,16,1024]{2,1,0:T(8,128)(2,1)} custom-call(bf16[128,16,1024]{2,1,0:T(8,128)(2,1)} %broadcast_select_fusion.1.x_ref), custom_call_target="tpu_custom_call" | custom-call | tf_op jit(solution)/shard_map/pallas_call | solution.py:51
  248.8 0.0 copy-start.2
  248.8 0.0 copy-start.4
  248.8 0.0 copy-start.5
  248.8 4.7 divide_convert_fusion
  253.5 0.0 copy-done.2
  253.5 0.0 copy-done.4
  253.5 0.0 copy-done.5
  253.5 3.1 fusion.1
  256.6 1.3 convolution_convert_fusion
  257.9 3.3 fusion.20
  261.2 9.6 %gather_fusion.4 = bf16[2048,1024]{1,0:T(8,128)(2,1)} fusion(bf16[512,1024]{1,0:T(8,128)(2,1)S(1)} %convolution_convert_fusion, s32[2048]{0:T(1024)S(1)} %fusion.16), kind=kCustom, calls=%fused_computation.1.clone | custom fusion | bytes 8396800 | tf_op jit(solution)/shard_map/jit(_take)/gather | solution.py:121
  270.8 4.2 multiply_convert_fusion.1
  274.9 85.4 %shard_map.105 = bf16[128,16,1024]{2,1,0:T(8,128)(2,1)} custom-call(bf16[128,16,1024]{2,1,0:T(8,128)(2,1)} %bitcast.34), custom_call_target="tpu_custom_call" | custom-call | tf_op jit(solution)/shard_map/pallas_call | solution.py:51
  360.3 3.4 fusion.11
  363.8 9.8 %gather_fusion.2 = f32[2048,1024]{1,0:T(8,128)} fusion(f32[256,1024]{1,0:T(8,128)S(1)} %fusion.11, s32[2048]{0:T(1024)S(1)} %broadcast_clamp_fusion), kind=kCustom, calls=%fused_computation.4 | custom fusion | bytes 16785408 | tf_op jit(solution)/shard_map/jit(_take)/gather | solution.py:131
  373.7 5.2 multiply_convert_fusion.x_ref
  378.9 0.0 copy-start.6
  378.9 77.8 %shard_map.106 = bf16[128,16,1024]{2,1,0:T(8,128)(2,1)} custom-call(bf16[128,16,1024]{2,1,0:T(8,128)(2,1)} %multiply_convert_fusion.x_ref), custom_call_target="tpu_custom_call" | custom-call | tf_op jit(solution)/shard_map/pallas_call | solution.py:51
  456.7 0.0 copy-done.6
  456.7 10.8 %convolution_bitcast_fusion = f32[2048,1024]{0,1:T(8,128)} fusion(bf16[512,2048]{1,0:T(8,128)(2,1)S(1)} %copy-done, bf16[512,1024]{1,0:T(8,128)(2,1)S(1)} %copy-done.6, f32[512,1024]{1,0:T(8,128)} %get-tuple-element.23, bf16[2048,1024]{1,0:T(8,128)(2,1)} %bitcast.36, s32[2048]{0:T(1024)S(1)} %eq.29), kind=kOutput, calls=%fused_computation.9 | convolution fusion | flops 4301783040 | bytes 17833984 | tf_op jit(solution)/shard_map/dot_general | solution.py:143
  467.5 122.9 %all-reduce.2 = (bf16[2048,1024]{0,1:T(8,128)(2,1)}, bf16[1024,1024]{1,0:T(8,128)(2,1)}) all-reduce(f32[2048,1024]{0,1:T(8,128)} %convolution_bitcast_fusion, f32[1024,1024]{1,0:T(8,128)} %fusion.20), channel_id=1, replica_groups=mesh['pin'=32,'board'=4] {'pin','board'}, use_global_device_ids=true, to_apply=%region_2.4 | all-reduce | flops 3145728 | bytes 18874368 | tf_op jit(solution)/shard_map/psum | solution.py:146
  590.5 6.4 %copy.34 = bf16[2048,1024]{1,0:T(8,128)(2,1)} copy(bf16[2048,1024]{0,1:T(8,128)(2,1)} %get-tuple-element.16) | data formatting | bytes 8388608
  (11 shorter events, 0.1 us)
Async XLA Ops:
  0.6 30.4 %copy-start = (bf16[512,2048]{1,0:T(8,128)(2,1)S(1)}, bf16[512,2048]{1,0:T(8,128)(2,1)}, u32[]{:S(2)}) copy-start(bf16[512,2048]{1,0:T(8,128)(2,1)} %param.10) | copy-start | bytes 6291460
  2.2 136.4 %all-to-all-start = ((s32[128,1,16]{2,1,0:T(1,128)}), s32[128,1,16]{2,1,0:T(1,128)S(1)}, u32[]{:S(2)}, u32[]{:S(2)}) async-start(s32[128,1,16]{2,1,0:T(1,128)} %bitcast.1), calls=%async_computation | async-start | bytes 131072 | tf_op jit(solution)/shard_map/all_to_all | solution.py:85
  17.0 13.2 %copy-start.3 = (s32[1,128]{1,0:T(1,128)S(1)}, s32[1,128]{1,0:T(1,128)}, u32[]{:S(2)}) copy-start(s32[1,128]{1,0:T(1,128)} %param.17) | copy-start | bytes 1540
  37.1 9.6 %copy-start.1 = (bf16[512,1024]{1,0:T(8,128)(2,1)}, bf16[512,1024]{1,0:T(8,128)(2,1)S(1)}, u32[]{:S(2)}) copy-start(bf16[512,1024]{1,0:T(8,128)(2,1)S(1)} %get-tuple-element.22) | copy-start | bytes 3145732
  138.6 13.6 %all-to-all-start.1 = ((s32[128,1,16]{2,1,0:T(1,128)}), s32[128,1,16]{2,1,0:T(1,128)S(1)}, u32[]{:S(2)}, u32[]{:S(2)}) async-start(s32[128,1,16]{2,1,0:T(1,128)} %compare_select_fusion), calls=%async_computation.1 | async-start | bytes 131072 | tf_op jit(solution)/shard_map/all_to_all | solution.py:86
  248.8 4.7 copy-start.2
  248.8 4.7 copy-start.4
  248.8 4.7 copy-start.5
  378.9 77.8 %copy-start.6 = (bf16[512,1024]{1,0:T(8,128)(2,1)S(1)}, bf16[512,1024]{1,0:T(8,128)(2,1)}, u32[]{:S(2)}) copy-start(bf16[512,1024]{1,0:T(8,128)(2,1)} %param.13) | copy-start | bytes 3145732

commit v2 on v0

v2 whole, which is shorter than its diff:
```python
import jax
import jax.numpy as jnp
from jax import lax
from jax.experimental import pallas as pl
from jax.experimental.pallas import tpu as pltpu
from jax.sharding import PartitionSpec as P

MESH = pl.DeviceIdType.MESH
BF = jnp.bfloat16
F32 = jnp.float32
DEV = 128
CAP = 16
SLOTS = DEV * CAP
PINS = 512
BOARDS = 256
F = 2048
H = 1024
W = 256
C = H // W
TILE = 512


def silu_slope(value):
    sig = jax.nn.sigmoid(value)
    return sig * (1.0 + value * (1.0 - sig))


def mm(a, b, dims=((1,), (0,))):
    return lax.dot_general(a, b, (dims, ((), ())), preferred_element_type=F32)


def iota(shape, axis):
    return lax.broadcasted_iota(jnp.int32, shape, axis)


def peer_of(step):
    pin = lax.axis_index("pin")
    board = lax.axis_index("board")
    dz = step % 4
    dx = (step // 4 + dz) % 4
    dy = (step // 16 + dx + dz) % 4
    dc = step // 64
    z, x, c = pin // 8, (pin // 2) % 4, pin % 2
    return ((z + dz) % 4) * 8 + ((x + dx) % 4) * 2 + (c + dc) % 2, (board + dy) % 4


def to_column(table):
    pick = (iota((SLOTS, DEV), 0) // CAP == iota((SLOTS, DEV), 1)).astype(F32).astype(BF)
    rows = mm(pick, table.astype(BF))
    keep = iota((SLOTS, DEV), 0) % CAP == iota((SLOTS, DEV), 1)
    return jnp.sum(jnp.where(keep, rows, 0.0), axis=1, keepdims=True)


def to_row(table):
    pick = (iota((DEV, SLOTS), 1) % CAP == iota((DEV, SLOTS), 0)).astype(F32).astype(BF)
    columns = mm(table.astype(BF), pick)
    keep = iota((DEV, SLOTS), 1) // CAP == iota((DEV, SLOTS), 0)
    return jnp.sum(jnp.where(keep, columns, 0.0), axis=0, keepdims=True)


def main_kernel(
    feat_hbm, wm_hbm, wu_hbm, cot_hbm, spin_ref, sboard_ref, swalk_ref, count_ref,
    out_hbm, gm_hbm, gu_hbm,
    feat, wm, wu, cot, out, gm, gu,
    pre, hid, s0, s1, ra, rb,
    pin_t, pin_m, pin_w, brd_t, brd_m, brd_w, feat_t,
    upd, dupd, nb, nb_t, scale_col, walk_col, pdeg, bdeg, brow_buf,
    table, idx_s, idx_r,
    load_sem, store_sem, idx_sem, send_sem, recv_sem,
):
    me = lax.axis_index("pin") * 4 + lax.axis_index("board")
    barrier = pltpu.get_barrier_semaphore()

    loads = [
        pltpu.make_async_copy(feat_hbm, feat, load_sem.at[0]),
        pltpu.make_async_copy(wm_hbm, wm, load_sem.at[1]),
        pltpu.make_async_copy(wu_hbm, wu, load_sem.at[2]),
        pltpu.make_async_copy(cot_hbm, cot, load_sem.at[3]),
    ]
    for load in loads:
        load.start()

    @pl.loop(1, DEV)
    def _(step):
        pl.semaphore_signal(barrier, inc=1, device_id=peer_of(step), device_id_type=MESH)

    diag = iota((DEV, DEV), 0) == iota((DEV, DEV), 1)
    count_col = jnp.sum(
        jnp.where(diag, jnp.broadcast_to(count_ref[...].astype(F32), (DEV, DEV)), 0.0), axis=1, keepdims=True
    )
    live = iota((DEV, CAP), 1).astype(F32) < count_col
    walks = jnp.where(live, swalk_ref[...], 0)
    table[...] = jnp.zeros_like(table)
    table[:, :CAP] = walks * 256 + sboard_ref[...]

    @pl.loop(0, DEV)
    def _(row):
        idx_s[row] = table[pl.ds(row, 1), :]

    table[...] = jnp.zeros_like(table)
    table[:, :CAP] = walks * 512 + spin_ref[...]
    packed = table[...]
    pin_hi = ((packed // 256) % 2).astype(F32)
    pin_lo = (packed % 256).astype(F32)
    walk_tab = (packed // 512).astype(F32)
    pin_col = to_column(pin_hi) * 256.0 + to_column(pin_lo)
    pin_t[...] = (iota((SLOTS, PINS), 1).astype(F32) == pin_col).astype(F32).astype(BF)

    pl.semaphore_wait(barrier, DEV - 1)

    own_idx = pltpu.make_async_copy(idx_s.at[me], idx_r.at[me], idx_sem.at[1])
    own_idx.start()

    @pl.loop(1, DEV)
    def _(step):
        pin, board = peer_of(step)
        pltpu.make_async_remote_copy(
            idx_s.at[pin * 4 + board], idx_r.at[me], idx_sem.at[0], idx_sem.at[1],
            device_id=(pin, board), device_id_type=MESH,
        ).start()

    def block(device):
        return pl.ds(pl.multiple_of(device * CAP, CAP), CAP)

    def send(phase, c, src, dst):
        pltpu.make_async_copy(src.at[c, block(me)], dst.at[c, block(me)], recv_sem.at[phase, c]).start()

        @pl.loop(1, DEV)
        def _(step):
            pin, board = peer_of(step)
            pltpu.make_async_remote_copy(
                src.at[c, block(pin * 4 + board)], dst.at[c, block(me)],
                send_sem.at[phase, c], recv_sem.at[phase, c],
                device_id=(pin, board), device_id_type=MESH,
            ).start()

    def wait_sent(phase, c, src):
        part = src.at[c, pl.ds(0, (DEV - 1) * CAP)]
        pltpu.make_async_copy(part, part, send_sem.at[phase, c]).wait()

    def wait_received(phase, c, dst):
        pltpu.make_async_copy(dst.at[c], dst.at[c], recv_sem.at[phase, c]).wait()

    def cols(c):
        return pl.ds(pl.multiple_of(c * W, W), W)

    def tile(i):
        return pl.ds(pl.multiple_of(i * TILE, TILE), TILE)

    loads[0].wait()
    loads[1].wait()

    @pl.loop(0, C)
    def _(c):
        value = mm(feat[...], wm[:, cols(c)])
        pre[:, cols(c)] = value
        hidden = (value * jax.nn.sigmoid(value)).astype(BF)
        hid[:, cols(c)] = hidden

        @pl.loop(0, SLOTS // TILE)
        def _(i):
            s0[c, tile(i)] = mm(pin_t[tile(i), :], hid[:, cols(c)]).astype(BF)

        send(0, c, s0, ra)

    pin_row = to_row(pin_hi) * 256.0 + to_row(pin_lo)
    walk_row = to_row(walk_tab)
    match = iota((PINS, SLOTS), 0).astype(F32) == pin_row
    pin_m[...] = match.astype(F32).astype(BF)
    weights = jnp.where(match, walk_row, 0.0)
    pin_w[...] = weights.astype(BF)
    pdeg[...] = jnp.maximum(jnp.sum(weights, axis=1, keepdims=True), 1.0)
    own_walk = to_column(walk_tab)
    degree_row = jnp.sum(pin_t[...].astype(F32) * own_walk, axis=0, keepdims=True)
    slot_degree = jnp.sum(pin_t[...].astype(F32) * degree_row, axis=1, keepdims=True)
    scale_col[...] = own_walk / jnp.maximum(slot_degree, 1.0)
    feat_t[...] = feat[...].T

    pltpu.make_async_copy(idx_r, idx_r, idx_sem.at[1]).wait()
    sent_idx = idx_s.at[pl.ds(0, DEV - 1)]
    pltpu.make_async_copy(sent_idx, sent_idx, idx_sem.at[0]).wait()

    @pl.loop(0, DEV)
    def _(row):
        table[pl.ds(row, 1), :] = idx_r[row]

    received = table[...]
    brd_tab = (received % 256).astype(F32)
    bwalk_tab = (received // 256).astype(F32)
    brd_t[...] = (iota((SLOTS, BOARDS), 1).astype(F32) == to_column(brd_tab)).astype(F32).astype(BF)
    walk_col[...] = to_column(bwalk_tab)
    match = iota((BOARDS, SLOTS), 0).astype(F32) == to_row(brd_tab)
    brd_m[...] = match.astype(F32).astype(BF)
    weights = jnp.where(match, to_row(bwalk_tab), 0.0)
    brd_w[...] = weights.astype(BF)
    bdeg[...] = jnp.maximum(jnp.sum(weights, axis=1, keepdims=True), 1.0)

    @pl.loop(0, C)
    def _(c):
        wait_received(0, c, ra)
        brow_buf[0] = (mm(brd_w[...], ra[c]) / bdeg[...]).astype(BF)

        @pl.loop(0, SLOTS // TILE)
        def _(i):
            s1[c, tile(i)] = mm(brd_t[tile(i), :], brow_buf[0]).astype(BF)

        send(1, c, s1, rb)

    loads[2].wait()
    loads[3].wait()
    upd[...] = jnp.zeros_like(upd)

    @pl.loop(0, C)
    def _(c):
        wait_received(1, c, rb)
        part = (mm(pin_w[...], rb[c]) / pdeg[...]).astype(BF)
        nb[:, cols(c)] = part

        @pl.loop(0, C)
        def _(n):
            upd[:, cols(n)] += mm(nb[:, cols(c)], wu[cols(c), cols(n)])

    @pl.loop(0, C)
    def _(n):
        update = upd[:, cols(n)]
        out[:, cols(n)] = (hid[:, cols(n)].astype(F32) + update * jax.nn.sigmoid(update)).astype(BF)
        dupd[:, cols(n)] = (cot[:, cols(n)].astype(F32) * silu_slope(update)).astype(BF)

    @pl.loop(0, C)
    def _(c):
        wait_sent(0, c, s0)
        brow_wide = mm(dupd[...], wu[cols(c), :], ((1,), (1,))).astype(BF)
        nb_t[0:PINS, 0:W] = brow_wide

        @pl.loop(0, SLOTS // TILE)
        def _(i):
            s0[c, tile(i)] = (scale_col[tile(i), :] * mm(pin_t[tile(i), :], nb_t[0:PINS, 0:W])).astype(BF)

        send(2, c, s0, ra)

    store_out = pltpu.make_async_copy(out, out_hbm, store_sem.at[0])
    store_out.start()
    nb_t[...] = nb[...].T

    @pl.loop(0, C)
    def _(n):
        gu[cols(n), :] = mm(nb_t[cols(n), :], dupd[...]).astype(BF)

    store_gu = pltpu.make_async_copy(gu, gu_hbm, store_sem.at[1])
    store_gu.start()

    @pl.loop(0, C)
    def _(c):
        wait_received(2, c, ra)
        wait_sent(1, c, s1)
        board_grad = mm(brd_m[...], ra[c]) / bdeg[...]
        high = board_grad.astype(BF)
        brow_buf[0] = high
        brow_buf[1] = (board_grad - high.astype(F32)).astype(BF)

        @pl.loop(0, SLOTS // TILE)
        def _(i):
            pick = brd_t[tile(i), :]
            rows = mm(pick, brow_buf[0]) + mm(pick, brow_buf[1])
            s1[c, tile(i)] = (walk_col[tile(i), :] * rows).astype(BF)

        send(3, c, s1, rb)

    @pl.loop(0, C)
    def _(c):
        wait_received(3, c, rb)
        grad = cot[:, cols(c)].astype(F32) + mm(pin_m[...], rb[c])
        d_pre = (grad * silu_slope(pre[:, cols(c)])).astype(BF)
        dupd[:, 0:W] = d_pre

        @pl.loop(0, F // TILE)
        def _(i):
            gm[tile(i), cols(c)] = mm(feat_t[tile(i), :], dupd[:, 0:W]).astype(BF)

    store_gm = pltpu.make_async_copy(gm, gm_hbm, store_sem.at[2])
    store_gm.start()

    @pl.loop(0, C)
    def _(c):
        wait_sent(2, c, s0)
        wait_sent(3, c, s1)

    store_out.wait()
    store_gu.wait()
    store_gm.wait()


def body(features, w_message, w_update, cotangent, slot_pin, slot_board, slot_walk, pair_count):
    hbm = pl.BlockSpec(memory_space=pl.ANY)
    vmem = pl.BlockSpec(memory_space=pltpu.VMEM)
    sem = pltpu.SemaphoreType.DMA
    output, gm, gu = pl.pallas_call(
        main_kernel,
        out_shape=(
            jax.ShapeDtypeStruct((PINS, H), BF),
            jax.ShapeDtypeStruct((F, H), BF),
            jax.ShapeDtypeStruct((H, H), BF),
        ),
        in_specs=[hbm] * 4 + [vmem] * 4,
        out_specs=(hbm, hbm, hbm),
        scratch_shapes=[
            pltpu.VMEM((PINS, F), BF), pltpu.VMEM((F, H), BF), pltpu.VMEM((H, H), BF), pltpu.VMEM((PINS, H), BF),
            pltpu.VMEM((PINS, H), BF), pltpu.VMEM((F, H), BF), pltpu.VMEM((H, H), BF),
            pltpu.VMEM((PINS, H), F32), pltpu.VMEM((PINS, H), BF),
            pltpu.VMEM((C, SLOTS, W), BF), pltpu.VMEM((C, SLOTS, W), BF),
            pltpu.VMEM((C, SLOTS, W), BF), pltpu.VMEM((C, SLOTS, W), BF),
            pltpu.VMEM((SLOTS, PINS), BF), pltpu.VMEM((PINS, SLOTS), BF), pltpu.VMEM((PINS, SLOTS), BF),
            pltpu.VMEM((SLOTS, BOARDS), BF), pltpu.VMEM((BOARDS, SLOTS), BF), pltpu.VMEM((BOARDS, SLOTS), BF),
            pltpu.VMEM((F, PINS), BF),
            pltpu.VMEM((PINS, H), F32), pltpu.VMEM((PINS, H), BF), pltpu.VMEM((PINS, H), BF), pltpu.VMEM((H, PINS), BF),
            pltpu.VMEM((SLOTS, 1), F32), pltpu.VMEM((SLOTS, 1), F32), pltpu.VMEM((PINS, 1), F32), pltpu.VMEM((BOARDS, 1), F32),
            pltpu.VMEM((2, BOARDS, W), BF),
            pltpu.VMEM((DEV, DEV), jnp.int32), pltpu.VMEM((DEV, 1, DEV), jnp.int32), pltpu.VMEM((DEV, 1, DEV), jnp.int32),
            sem((4,)), sem((3,)), sem((2,)), sem((4, C)), sem((4, C)),
        ],
        name="layer",
        compiler_params=pltpu.CompilerParams(
            collective_id=0, has_side_effects=True, vmem_limit_bytes=62 * 1024 * 1024
        ),
    )(
        features, w_message, w_update, cotangent,
        slot_pin[0], slot_board[0], slot_walk[0], pair_count,
    )
    wide = lax.optimization_barrier((gm.astype(F32), gu.astype(F32)))
    total_message, total_update = lax.psum(wide, ("pin", "board"))
    return (output, total_message.astype(BF), total_update.astype(BF))


def solution(mesh):
    in_specs = (
        P(("pin", "board"), None),
        P(),
        P(),
        P(("pin", "board"), None),
        P(("pin", "board"), None, None),
        P(("pin", "board"), None, None),
        P(("pin", "board"), None, None),
        P(("pin", "board"), None),
    )
    out_specs = (P(("pin", "board"), None), P(), P())
    return jax.shard_map(body, mesh=mesh, in_specs=in_specs, out_specs=out_specs, check_vma=False)
```

time: 492 us -> 353 us (0.72)
  Pallas kernels: 0 us -> 219 us
  waiting for transfers between devices: 209 us -> 0 us
  local copies, waits for them, and re-layouts: 63.1 us -> 5.25 us
  starting transfers between devices: 41.4 us -> 0 us
  matrix products: 37.5 us -> 0 us
  other arithmetic: 21.3 us -> 8.41 us
    pallas_call x0 -> x1, Pallas kernels: none -> 219 us  [body(): pl.pallas_call(main_kernel, out_shape=(jax.ShapeDtypeStruct((PINS, H), BF...]
    all_to_all x6 -> x0, waiting for transfers between devices: 209 us -> none  [the longest x1 52.5 us: body(): lax.all_to_all(slot_grad, ('pin', 'board'), split_axis=0, concat_axis=0,...]
    gather x5 -> x0, local copies, waits for them, and re-layouts: 51.9 us -> none  [the longest x1 13.2 us: body(): jnp.take(pin_degree, pins_flat, axis=0)]
    all_to_all x6 -> x0, starting transfers between devices: 41.4 us -> none  [the longest x1 11.5 us: body(): lax.all_to_all(walks_int, ('pin', 'board'), split_axis=0, concat_axis=0,...]
    dot_general x8 -> x0, matrix products: 37.5 us -> none  [the longest x1 11.1 us: body(): lax.dot_general(features, d_pre, (((0,), (0,)), ((), ())), preferred_elem...]
    select_n x5 -> x0, other arithmetic: 9.26 us -> none  [the longest x2 3.88 us: body(): jnp.take(board_rows, recv_board_flat, axis=0)]
    unnamed x22 -> x8, local copies, waits for them, and re-layouts: 10 us -> 5.25 us
  transfers between devices with their start and end apart: 6 -> 0, of which waited for: 5 -> 0; matrix products, arithmetic and copies ran while one was open for 9% -> 0% of each run, Pallas kernels for 0% -> 0%
where the time goes in v2:
time: 353 us; the launch traced here: 352 us
  Pallas kernels  219 us (62%)
  blocking collectives  119 us (34%)
  other arithmetic  8.41 us (2%)
  local copies, waits for them, and re-layouts  5.25 us (1%)
    pallas_call x1, Pallas kernels, body(): pl.pallas_call(main_kernel, out_shape=(jax.ShapeDtypeStruct((PINS, H), BF...  219 us
    psum x1, blocking collectives, body(): total_message, total_update = lax.psum(wide, ('pin', 'board'))  119 us
    convert_element_type x2, other arithmetic, body(): wide = lax.optimization_barrier((gm.astype(F32), gu.astype(F32)))  8.41 us

profile of v2, /device:TPU:1, one launch (start us, length us, event | category | flops | bytes accessed | tf_op | source)
XLA Modules:
  0.0 352.2 jit_solution(12497537731976480322)
XLA Ops:
  0.6 1.4 copy.11
  2.1 1.4 copy.12
  3.5 1.4 copy.13
  4.9 219.2 %layer.1 = (bf16[512,1024]{1,0:T(8,128)(2,1)}, bf16[2048,1024]{1,0:T(8,128)(2,1)}, bf16[1024,1024]{1,0:T(8,128)(2,1)}) custom-call(bf16[512,2048]{1,0:T(8,128)(2,1)} %feat_hbm.1, bf16[2048,1024]{1,0:T(8,128)(2,1)} %wm_hbm.1, bf16[1024,1024]{1,0:T(8,128)(2,1)} %wu_hbm.1, bf16[512,1024]{1,0:T(8,128)(2,1)} %cot_hbm.1, s32[128,16]{1,0:T(8,128)} %bitcast.3, ...), custom_call_target="tpu_custom_call" | custom-call | tf_op jit(solution)/shard_map/layer/pallas_call | solution.py:297
  224.1 0.0 copy-start
  224.1 4.2 %convert_element_type.13 = f32[1024,1024]{1,0:T(8,128)} convert(bf16[1024,1024]{1,0:T(8,128)(2,1)} %get-tuple-element.10) | non-fusion elementwise | flops 1048576 | bytes 6291456 | tf_op jit(solution)/shard_map/convert_element_type | solution.py:329
  228.2 0.0 copy-done
  228.3 4.2 %convert_element_type.12 = f32[2048,1024]{1,0:T(8,128)} convert(bf16[2048,1024]{1,0:T(8,128)(2,1)S(1)} %copy-done) | non-fusion elementwise | flops 2097152 | bytes 12582912 | tf_op jit(solution)/shard_map/convert_element_type | solution.py:329
  232.5 0.0 copy-start.1
  232.5 118.7 %all-reduce.2 = (bf16[2048,1024]{1,0:T(8,128)(2,1)}, bf16[1024,1024]{1,0:T(8,128)(2,1)}) all-reduce(f32[2048,1024]{1,0:T(8,128)} %convert_element_type.12, f32[1024,1024]{1,0:T(8,128)} %convert_element_type.13), channel_id=1, replica_groups=mesh['pin'=32,'board'=4] {'pin','board'}, use_global_device_ids=true, to_apply=%region_0.0 | all-reduce | flops 3145728 | bytes 18874368 | tf_op jit(solution)/shard_map/psum | solution.py:330
  351.2 0.0 copy-done.1
  351.3 1.0 copy.19
Async XLA Ops:
  224.1 4.2 %copy-start = (bf16[2048,1024]{1,0:T(8,128)(2,1)S(1)}, bf16[2048,1024]{1,0:T(8,128)(2,1)}, u32[]{:S(2)}) copy-start(bf16[2048,1024]{1,0:T(8,128)(2,1)} %get-tuple-element.9) | copy-start | bytes 12582916
  232.5 118.8 %copy-start.1 = (bf16[512,1024]{1,0:T(8,128)(2,1)S(1)}, bf16[512,1024]{1,0:T(8,128)(2,1)}, u32[]{:S(2)}) copy-start(bf16[512,1024]{1,0:T(8,128)(2,1)} %get-tuple-element.18) | copy-start | bytes 3145732

commit v3 on v2

v3 whole, which is shorter than its diff:
```python
import jax
import jax.numpy as jnp
from jax import lax
from jax.experimental import pallas as pl
from jax.experimental.pallas import tpu as pltpu
from jax.sharding import PartitionSpec as P

MESH = pl.DeviceIdType.MESH
BF = jnp.bfloat16
F32 = jnp.float32
DEV = 128
CAP = 16
SLOTS = DEV * CAP
PINS = 512
BOARDS = 256
F = 2048
H = 1024
W = 256
C = H // W
TILE = 512


def silu_slope(value):
    sig = jax.nn.sigmoid(value)
    return sig * (1.0 + value * (1.0 - sig))


def mm(a, b, dims=((1,), (0,))):
    return lax.dot_general(a, b, (dims, ((), ())), preferred_element_type=F32)


def iota(shape, axis):
    return lax.broadcasted_iota(jnp.int32, shape, axis)


def peer_of(step):
    pin = lax.axis_index("pin")
    board = lax.axis_index("board")
    dz = step % 4
    dx = (step // 4 + dz) % 4
    dy = (step // 16 + dx + dz) % 4
    dc = step // 64
    z, x, c = pin // 8, (pin // 2) % 4, pin % 2
    return ((z + dz) % 4) * 8 + ((x + dx) % 4) * 2 + (c + dc) % 2, (board + dy) % 4


def relative(axis, step):
    pin = lax.axis_index("pin")
    place = [pin // 8, (pin // 2) % 4, lax.axis_index("board")]
    if isinstance(step, int):
        place[axis] = (place[axis] + step) % 4
    else:
        b, d = (axis + 1) % 3, (axis + 2) % 3
        place[b] = (place[b] + step // 4) % 4
        place[d] = (place[d] + step) % 4
        rank = place[b] * 4 + place[d]
        return (place[0] * 8 + place[1] * 2 + pin % 2, place[2]), rank
    return (place[0] * 8 + place[1] * 2 + pin % 2, place[2]), place[axis]


def grad_steps(src, dst, row0, c, buf, brow0, axis, send_sem, recv_sem):
    pin = lax.axis_index("pin")
    core = pin % 2
    partner = (pin + 1 - 2 * core, lax.axis_index("board"))
    quarter = relative(axis, 0)[1]
    rank = relative(axis, jnp.int32(0))[1]
    half = W // 2
    own = pl.ds(pl.multiple_of(c * W + core * half, half), half)
    other = pl.ds(pl.multiple_of(c * W + (1 - core) * half, half), half)
    left, right = pl.ds(0, half), pl.ds(half, half)
    every = pl.ds(row0, 1024)
    pair_buf = buf.at[pl.ds(brow0, 1024), left]
    line_buf = buf.at[pl.ds(brow0, 768), right]
    plane_buf = buf.at[pl.ds(brow0 + 768, 240), right]

    def line_rows(q):
        return pl.ds(pl.multiple_of(row0 + q * 256, 256), 256)

    def plane_rows(r):
        return pl.ds(pl.multiple_of(row0 + quarter * 256 + r * 16, 16), 16)

    def put(a, b, step, device):
        pltpu.make_async_remote_copy(
            a, b, send_sem.at[step], recv_sem.at[step], device_id=device, device_id_type=MESH
        ).start()

    def arrived(like, step):
        pltpu.make_async_copy(like, like, recv_sem.at[step]).wait()

    def pair_out():
        put(src.at[every, other], pair_buf, 0, partner)

    def line_out():
        arrived(pair_buf, 0)
        src[every, own] = (src[every, own].astype(F32) + pair_buf[...].astype(F32)).astype(BF)
        for dq in (1, 3, 2):
            device, q = relative(axis, dq)
            put(src.at[line_rows(q), own], buf.at[pl.ds(brow0 + (dq - 1) * 256, 256), right], 1, device)

    def plane_out():
        arrived(line_buf, 1)
        total = src[line_rows(quarter), own].astype(F32)
        for i in range(3):
            total += buf[brow0 + i * 256:brow0 + (i + 1) * 256, half:].astype(F32)
        src[line_rows(quarter), own] = total.astype(BF)

        @pl.loop(1, 16)
        def _(step):
            device, r = relative(axis, step)
            put(
                src.at[plane_rows(r), own],
                buf.at[pl.ds(pl.multiple_of(brow0 + 752 + step * 16, 16), 16), right],
                2, device,
            )

    def plane_back():
        arrived(plane_buf, 2)
        parts = plane_buf[...].astype(F32).reshape(15, 16, half)
        total = src[plane_rows(rank), own].astype(F32) + jnp.sum(parts, axis=0)
        dst[plane_rows(rank), own] = total.astype(BF)

        @pl.loop(1, 16)
        def _(step):
            device, _ = relative(axis, step)
            piece = dst.at[plane_rows(rank), own]
            put(piece, piece, 3, device)

    def line_back():
        arrived(plane_buf, 3)
        piece = dst.at[line_rows(quarter), own]
        for dq in (1, 3, 2):
            put(piece, piece, 4, relative(axis, dq)[0])

    def pair_back():
        arrived(line_buf, 4)
        piece = dst.at[every, own]
        put(piece, piece, 5, partner)

    def finish():
        arrived(pair_buf, 5)

    def sent():
        for step, like in enumerate((pair_buf, line_buf, plane_buf, plane_buf, line_buf, pair_buf)):
            pltpu.make_async_copy(like, like, send_sem.at[step]).wait()

    return [pair_out, line_out, plane_out, plane_back, line_back, pair_back, finish, sent]


def to_column(table):
    pick = (iota((SLOTS, DEV), 0) // CAP == iota((SLOTS, DEV), 1)).astype(F32).astype(BF)
    rows = mm(pick, table.astype(BF))
    keep = iota((SLOTS, DEV), 0) % CAP == iota((SLOTS, DEV), 1)
    return jnp.sum(jnp.where(keep, rows, 0.0), axis=1, keepdims=True)


def to_row(table):
    pick = (iota((DEV, SLOTS), 1) % CAP == iota((DEV, SLOTS), 0)).astype(F32).astype(BF)
    columns = mm(table.astype(BF), pick)
    keep = iota((DEV, SLOTS), 1) // CAP == iota((DEV, SLOTS), 0)
    return jnp.sum(jnp.where(keep, columns, 0.0), axis=0, keepdims=True)


def main_kernel(
    feat_hbm, wm_hbm, wu_hbm, cot_hbm, spin_ref, sboard_ref, swalk_ref, count_ref,
    out, gm, gu,
    feat, wm, wu, cot,
    pre, hid, s0, s1, ra, rb,
    pin_t, pin_w, brd_t, brd_w, feat_t,
    upd, nb_t, scale_col, walk_col, pdeg, bdeg, brow_buf, grad_buf, small,
    table, idx_s, idx_r,
    load_sem, idx_sem, send_sem, recv_sem, gsend_sem, grecv_sem,
):
    me = lax.axis_index("pin") * 4 + lax.axis_index("board")
    barrier = pltpu.get_barrier_semaphore()

    loads = [
        pltpu.make_async_copy(feat_hbm, feat, load_sem.at[0]),
        pltpu.make_async_copy(wm_hbm, wm, load_sem.at[1]),
        pltpu.make_async_copy(wu_hbm, wu, load_sem.at[2]),
        pltpu.make_async_copy(cot_hbm, cot, load_sem.at[3]),
    ]
    for load in loads:
        load.start()

    @pl.loop(1, DEV)
    def _(step):
        pl.semaphore_signal(barrier, inc=1, device_id=peer_of(step), device_id_type=MESH)

    def block(device):
        return pl.ds(pl.multiple_of(device * CAP, CAP), CAP)

    def send(phase, c, src, dst):
        pltpu.make_async_copy(src.at[c, block(me)], dst.at[c, block(me)], recv_sem.at[phase, c]).start()

        @pl.loop(1, DEV)
        def _(step):
            pin, board = peer_of(step)
            pltpu.make_async_remote_copy(
                src.at[c, block(pin * 4 + board)], dst.at[c, block(me)],
                send_sem.at[phase, c], recv_sem.at[phase, c],
                device_id=(pin, board), device_id_type=MESH,
            ).start()

    def wait_sent(phase, c, src):
        part = src.at[c, pl.ds(0, (DEV - 1) * CAP)]
        pltpu.make_async_copy(part, part, send_sem.at[phase, c]).wait()

    def wait_received(phase, c, dst):
        pltpu.make_async_copy(dst.at[c], dst.at[c], recv_sem.at[phase, c]).wait()

    def cols(c):
        return pl.ds(pl.multiple_of(c * W, W), W)

    def tile(i):
        return pl.ds(pl.multiple_of(i * TILE, TILE), TILE)

    live = iota((CAP, DEV), 0) < count_ref[...]
    walks = jnp.where(live, swalk_ref[...], 0)
    table[...] = jnp.zeros_like(table)
    table[:CAP, :] = (walks * 512 + spin_ref[...]).astype(F32)
    packed = table[...].T.astype(jnp.int32)
    pin_hi = ((packed // 256) % 2).astype(F32)
    pin_lo = (packed % 256).astype(F32)
    walk_tab = (packed // 512).astype(F32)
    pin_col = to_column(pin_hi) * 256.0 + to_column(pin_lo)
    pin_t[...] = (iota((SLOTS, PINS), 1).astype(F32) == pin_col).astype(F32).astype(BF)
    loads[0].wait()
    loads[1].wait()

    def project(c):
        value = mm(feat[...], wm[:, cols(c)])
        pre[:, cols(c)] = value
        hid[:, cols(c)] = (value * jax.nn.sigmoid(value)).astype(BF)

        @pl.loop(0, SLOTS // TILE)
        def _(i):
            s0[c, tile(i)] = mm(pin_t[tile(i), :], hid[:, cols(c)]).astype(BF)

    project(0)
    pl.semaphore_wait(barrier, DEV - 1)
    send(0, 0, s0, ra)

    table[:CAP, :] = (walks * 256 + sboard_ref[...]).astype(F32)
    table[...] = table[...].T

    @pl.loop(0, DEV)
    def _(row):
        idx_s[row] = table[pl.ds(row, 1), :].astype(jnp.int32)

    pltpu.make_async_copy(idx_s.at[me], idx_r.at[me], idx_sem.at[1]).start()

    @pl.loop(1, DEV)
    def _(step):
        pin, board = peer_of(step)
        pltpu.make_async_remote_copy(
            idx_s.at[pin * 4 + board], idx_r.at[me], idx_sem.at[0], idx_sem.at[1],
            device_id=(pin, board), device_id_type=MESH,
        ).start()

    @pl.loop(1, C)
    def _(c):
        project(c)
        send(0, c, s0, ra)

    pin_row = to_row(pin_hi) * 256.0 + to_row(pin_lo)
    walk_row = to_row(walk_tab)
    match = iota((PINS, SLOTS), 0).astype(F32) == pin_row
    weights = jnp.where(match, walk_row, 0.0)
    pin_w[...] = weights.astype(BF)
    pdeg[...] = jnp.maximum(jnp.sum(weights, axis=1, keepdims=True), 1.0)
    own_walk = to_column(walk_tab)
    degree_row = jnp.sum(pin_t[...].astype(F32) * own_walk, axis=0, keepdims=True)
    slot_degree = jnp.sum(pin_t[...].astype(F32) * degree_row, axis=1, keepdims=True)
    scale_col[...] = own_walk / jnp.maximum(slot_degree, 1.0)
    feat_t[...] = feat[...].T

    pltpu.make_async_copy(idx_r, idx_r, idx_sem.at[1]).wait()
    sent_idx = idx_s.at[pl.ds(0, DEV - 1)]
    pltpu.make_async_copy(sent_idx, sent_idx, idx_sem.at[0]).wait()

    @pl.loop(0, DEV)
    def _(row):
        table[pl.ds(row, 1), :] = idx_r[row].astype(F32)

    received = table[...].astype(jnp.int32)
    brd_tab = (received % 256).astype(F32)
    bwalk_tab = (received // 256).astype(F32)
    brd_t[...] = (iota((SLOTS, BOARDS), 1).astype(F32) == to_column(brd_tab)).astype(F32).astype(BF)
    walk_col[...] = to_column(bwalk_tab)
    match = iota((BOARDS, SLOTS), 0).astype(F32) == to_row(brd_tab)
    weights = jnp.where(match, to_row(bwalk_tab), 0.0)
    brd_w[...] = weights.astype(BF)
    bdeg[...] = jnp.maximum(jnp.sum(weights, axis=1, keepdims=True), 1.0)

    @pl.loop(0, C)
    def _(c):
        wait_received(0, c, ra)
        brow_buf[0] = (mm(brd_w[...], ra[c]) / bdeg[...]).astype(BF)

        @pl.loop(0, SLOTS // TILE)
        def _(i):
            s1[c, tile(i)] = mm(brd_t[tile(i), :], brow_buf[0]).astype(BF)

        send(1, c, s1, rb)

    brd_w[...] = (brd_w[...].astype(F32) > 0.0).astype(F32).astype(BF)
    loads[2].wait()
    loads[3].wait()
    upd[...] = jnp.zeros_like(upd)

    @pl.loop(0, C)
    def _(c):
        wait_received(1, c, rb)
        part = (mm(pin_w[...], rb[c]) / pdeg[...]).astype(BF)
        small[...] = part
        nb_t[cols(c), :] = part.T

        @pl.loop(0, C)
        def _(n):
            upd[:, cols(n)] += mm(small[...], wu[cols(c), cols(n)])

    @pl.loop(0, C)
    def _(n):
        feat[:, cols(n)] = (cot[:, cols(n)].astype(F32) * silu_slope(upd[:, cols(n)])).astype(BF)

    @pl.loop(0, C)
    def _(c):
        wait_sent(0, c, s0)
        small[...] = mm(feat[:, :H], wu[cols(c), :], ((1,), (1,))).astype(BF)

        @pl.loop(0, SLOTS // TILE)
        def _(i):
            s0[c, tile(i)] = (scale_col[tile(i), :] * mm(pin_t[tile(i), :], small[...])).astype(BF)

        send(2, c, s0, ra)

    @pl.loop(0, C)
    def _(n):
        wu[cols(n), :] = mm(nb_t[cols(n), :], feat[:, :H]).astype(BF)

    update_steps = [
        grad_steps(wu, gu, 0, i, grad_buf.at[i // 2], (i % 2) * 1024, i % 3, gsend_sem.at[i], grecv_sem.at[i])
        for i in range(4)
    ]
    for steps in update_steps:
        steps[0]()

    @pl.loop(0, C)
    def _(n):
        update = upd[:, cols(n)]
        out[:, cols(n)] = (hid[:, cols(n)].astype(F32) + update * jax.nn.sigmoid(update)).astype(BF)

    pin_w[...] = (pin_w[...].astype(F32) > 0.0).astype(F32).astype(BF)

    for c in range(C):
        wait_received(2, c, ra)
        wait_sent(1, c, s1)
        board_grad = mm(brd_w[...], ra[c]) / bdeg[...]
        high = board_grad.astype(BF)
        brow_buf[0] = high
        brow_buf[1] = (board_grad - high.astype(F32)).astype(BF)

        @pl.loop(0, SLOTS // TILE)
        def _(i):
            pick = brd_t[tile(i), :]
            rows = mm(pick, brow_buf[0]) + mm(pick, brow_buf[1])
            s1[c, tile(i)] = (walk_col[tile(i), :] * rows).astype(BF)

        send(3, c, s1, rb)
        for steps in update_steps:
            steps[1 + c]()

    message_steps = []
    for c in range(C):
        wait_received(3, c, rb)
        grad = cot[:, cols(c)].astype(F32) + mm(pin_w[...], rb[c])
        small[...] = (grad * silu_slope(pre[:, cols(c)])).astype(BF)

        @pl.loop(0, F // TILE)
        def _(i):
            wm[tile(i), cols(c)] = mm(feat_t[tile(i), :], small[...]).astype(BF)

        message_steps.append([
            grad_steps(
                wm, gm, h * 1024, c, ra.at[c], h * 1024, (2 * c + h) % 3,
                gsend_sem.at[4 + 2 * c + h], grecv_sem.at[4 + 2 * c + h],
            )
            for h in range(2)
        ])
        if c < 2:
            for steps in update_steps:
                steps[5 + c]()
        for back in range(c + 1):
            for steps in message_steps[c - back]:
                steps[back]()

    for tick in range(1, 7):
        for back in range(tick, min(tick + C, 7)):
            for steps in message_steps[C - 1 + tick - back]:
                steps[back]()

    @pl.loop(0, C)
    def _(c):
        wait_sent(2, c, s0)
        wait_sent(3, c, s1)

    for steps in update_steps + message_steps[0] + message_steps[1] + message_steps[2] + message_steps[3]:
        steps[7]()


def body(features, w_message, w_update, cotangent, slot_pin, slot_board, slot_walk, pair_count):
    hbm = pl.BlockSpec(memory_space=pl.ANY)
    vmem = pl.BlockSpec(memory_space=pltpu.VMEM)
    sem = pltpu.SemaphoreType.DMA
    output, gm, gu = pl.pallas_call(
        main_kernel,
        out_shape=(
            jax.ShapeDtypeStruct((PINS, H), BF),
            jax.ShapeDtypeStruct((F, H), BF),
            jax.ShapeDtypeStruct((H, H), BF),
        ),
        in_specs=[hbm] * 4 + [vmem] * 4,
        out_specs=(vmem, vmem, vmem),
        scratch_shapes=[
            pltpu.VMEM((PINS, F), BF), pltpu.VMEM((F, H), BF), pltpu.VMEM((H, H), BF), pltpu.VMEM((PINS, H), BF),
            pltpu.VMEM((PINS, H), F32), pltpu.VMEM((PINS, H), BF),
            pltpu.VMEM((C, SLOTS, W), BF), pltpu.VMEM((C, SLOTS, W), BF),
            pltpu.VMEM((C, SLOTS, W), BF), pltpu.VMEM((C, SLOTS, W), BF),
            pltpu.VMEM((SLOTS, PINS), BF), pltpu.VMEM((PINS, SLOTS), BF),
            pltpu.VMEM((SLOTS, BOARDS), BF), pltpu.VMEM((BOARDS, SLOTS), BF),
            pltpu.VMEM((F, PINS), BF),
            pltpu.VMEM((PINS, H), F32), pltpu.VMEM((H, PINS), BF),
            pltpu.VMEM((SLOTS, 1), F32), pltpu.VMEM((SLOTS, 1), F32), pltpu.VMEM((PINS, 1), F32), pltpu.VMEM((BOARDS, 1), F32),
            pltpu.VMEM((2, BOARDS, W), BF), pltpu.VMEM((2, SLOTS, W), BF), pltpu.VMEM((PINS, W), BF),
            pltpu.VMEM((DEV, DEV), F32), pltpu.VMEM((DEV, 1, DEV), jnp.int32), pltpu.VMEM((DEV, 1, DEV), jnp.int32),
            sem((4,)), sem((2,)), sem((4, C)), sem((4, C)), sem((12, 6)), sem((12, 6)),
        ],
        name="layer",
        compiler_params=pltpu.CompilerParams(
            collective_id=0, has_side_effects=True, vmem_limit_bytes=62 * 1024 * 1024
        ),
    )(
        features, w_message, w_update, cotangent,
        slot_pin[0].T, slot_board[0].T, slot_walk[0].T, pair_count,
    )
    return output, gm, gu


def solution(mesh):
    in_specs = (
        P(("pin", "board"), None),
        P(),
        P(),
        P(("pin", "board"), None),
        P(("pin", "board"), None, None),
        P(("pin", "board"), None, None),
        P(("pin", "board"), None, None),
        P(("pin", "board"), None),
    )
    out_specs = (P(("pin", "board"), None), P(), P())
    return jax.shard_map(body, mesh=mesh, in_specs=in_specs, out_specs=out_specs, check_vma=False)
```

time: 353 us -> 281 us (0.80)
  blocking collectives: 119 us -> 0 us
  Pallas kernels: 219 us -> 272 us
  other arithmetic: 8.41 us -> 0 us
    psum x1 -> x0, blocking collectives: 119 us -> none  [body(): total_message, total_update = lax.psum(wide, ('pin', 'board'))]
    pallas_call x1, Pallas kernels: 219 us -> 272 us  [body(): pl.pallas_call(main_kernel, out_shape=(jax.ShapeDtypeStruct((PINS, H), BF...]
    convert_element_type x2 -> x0, other arithmetic: 8.41 us -> none  [body(): wide = lax.optimization_barrier((gm.astype(F32), gu.astype(F32)))]
    unnamed x8 -> x5, local copies, waits for them, and re-layouts: 5.25 us -> 8.37 us
where the time goes in v3:
time: 281 us
  Pallas kernels  272 us (97%)
  local copies, waits for them, and re-layouts  8.37 us (3%)
    pallas_call x1, Pallas kernels, body(): pl.pallas_call(main_kernel, out_shape=(jax.ShapeDtypeStruct((PINS, H), BF...  272 us
    unnamed x5, local copies, waits for them, and re-layouts  8.37 us

profile of v3, /device:TPU:1, one launch (start us, length us, event | category | flops | bytes accessed | tf_op | source)
XLA Modules:
  0.0 280.8 jit_solution(9219414324279568722)
XLA Ops:
  0.6 271.8 %layer.1 = (bf16[512,1024]{1,0:T(8,128)(2,1)}, bf16[2048,1024]{1,0:T(8,128)(2,1)}, bf16[1024,1024]{1,0:T(8,128)(2,1)}) custom-call(bf16[512,2048]{1,0:T(8,128)(2,1)} %feat_hbm.1, bf16[2048,1024]{1,0:T(8,128)(2,1)} %wm_hbm.1, bf16[1024,1024]{1,0:T(8,128)(2,1)} %wu_hbm.1, bf16[512,1024]{1,0:T(8,128)(2,1)} %cot_hbm.1, s32[16,128]{1,0:T(8,128)} %bitcast.9, ...), custom_call_target="tpu_custom_call" | custom-call | tf_op jit(solution)/shard_map/layer/pallas_call | solution.py:415
  272.4 2.3 copy.14
  274.7 0.0 copy-start
  274.7 4.8 %copy.15 = bf16[2048,1024]{1,0:T(8,128)(2,1)} copy(bf16[2048,1024]{1,0:T(8,128)(2,1)} %get-tuple-element.7) | data formatting | bytes 8388608
  279.5 0.0 copy-done
  279.5 1.3 copy.16
Async XLA Ops:
  274.7 4.8 %copy-start = (bf16[1024,1024]{1,0:T(8,128)(2,1)S(1)}, bf16[1024,1024]{1,0:T(8,128)(2,1)}, u32[]{:S(2)}) copy-start(bf16[1024,1024]{1,0:T(8,128)(2,1)} %get-tuple-element.8) | copy-start | bytes 6291460

commit v4 on v3

--- a/solution.py
+++ b/solution.py
@@ -33,37 +33,72 @@
     return lax.broadcasted_iota(jnp.int32, shape, axis)
 
 
-def peer_of(step):
+def places():
     pin = lax.axis_index("pin")
-    board = lax.axis_index("board")
-    dz = step % 4
-    dx = (step // 4 + dz) % 4
-    dy = (step // 16 + dx + dz) % 4
-    dc = step // 64
-    z, x, c = pin // 8, (pin // 2) % 4, pin % 2
-    return ((z + dz) % 4) * 8 + ((x + dx) % 4) * 2 + (c + dc) % 2, (board + dy) % 4
-
-
-def relative(axis, step):
-    pin = lax.axis_index("pin")
-    place = [pin // 8, (pin // 2) % 4, lax.axis_index("board")]
-    if isinstance(step, int):
-        place[axis] = (place[axis] + step) % 4
-    else:
-        b, d = (axis + 1) % 3, (axis + 2) % 3
-        place[b] = (place[b] + step // 4) % 4
-        place[d] = (place[d] + step) % 4
-        rank = place[b] * 4 + place[d]
-        return (place[0] * 8 + place[1] * 2 + pin % 2, place[2]), rank
-    return (place[0] * 8 + place[1] * 2 + pin % 2, place[2]), place[axis]
+    z, x, y = lax.div(pin, 8), lax.rem(lax.div(pin, 2), 4), lax.axis_index("board")
+    zs = [lax.rem(z + i, 4) * 8 for i in range(4)]
+    xs = [lax.rem(x + i, 4) * 2 for i in range(4)]
+    ys = [lax.rem(y + i, 4) for i in range(4)]
+    return zs, xs, lax.rem(pin, 2), ys
+
+
+def for_peers(visit):
+    zs, xs, core, ys = places()
+
+    def group(step, first):
+        dc, dy = lax.div(step, 4), lax.rem(step, 4)
+        c = lax.rem(core + dc, 2)
+        rows = [lax.rem(ys[i] + dy, 4) for i in range(4)]
+        for i in range(4):
+            for dz in range(4):
+                if first and i == 0 and dz == 0:
+                    continue
+                dx = (i + dz) % 4
+                visit((zs[dz] + xs[dx] + c, rows[(dx + dz) % 4]))
+
+    group(jnp.int32(0), True)
+
+    @pl.loop(1, 8)
+    def _(step):
+        group(step, False)
+
+
+def line_of(axis):
+    zs, xs, core, ys = places()
+    tables, scale = [zs, xs, ys], (8, 2, 1)[axis]
+    others = []
+    for i in (1, 3, 2):
+        place = [zs[0], xs[0], ys[0]]
+        place[axis] = tables[axis][i]
+        others.append(((place[0] + place[1] + core, place[2]), lax.div(place[axis], scale), i - 1))
+    return lax.div(tables[axis][0], scale), others
+
+
+def plane_of(axis):
+    zs, xs, core, ys = places()
+    tables, scales = [zs, xs, ys], (8, 2, 1)
+    b, d = (axis + 1) % 3, (axis + 2) % 3
+    rb = [lax.div(v, scales[b]) * 4 for v in tables[b]]
+    rd = [lax.div(v, scales[d]) for v in tables[d]]
+    others = []
+    for i in range(4):
+        for j in range(4):
+            if i or j:
+                k, m = i, (i + j) % 4
+                if not (k or m):
+                    continue
+                place = [zs[0], xs[0], ys[0]]
+                place[b], place[d] = tables[b][k], tables[d][m]
+                others.append(((place[0] + place[1] + core, place[2]), rb[k] + rd[m], 4 * k + m - 1))
+    return rb[0] + rd[0], others
 
 
 def grad_steps(src, dst, row0, c, buf, brow0, axis, send_sem, recv_sem):
     pin = lax.axis_index("pin")
-    core = pin % 2
+    core = lax.rem(pin, 2)
     partner = (pin + 1 - 2 * core, lax.axis_index("board"))
-    quarter = relative(axis, 0)[1]
-    rank = relative(axis, jnp.int32(0))[1]
+    quarter, line = line_of(axis)
+    rank, plane = plane_of(axis)
     half = W // 2
     own = pl.ds(pl.multiple_of(c * W + core * half, half), half)
     other = pl.ds(pl.multiple_of(c * W + (1 - core) * half, half), half)
@@ -93,9 +128,8 @@
     def line_out():
         arrived(pair_buf, 0)
         src[every, own] = (src[every, own].astype(F32) + pair_buf[...].astype(F32)).astype(BF)
-        for dq in (1, 3, 2):
-            device, q = relative(axis, dq)
-            put(src.at[line_rows(q), own], buf.at[pl.ds(brow0 + (dq - 1) * 256, 256), right], 1, device)
+        for device, q, slot in line:
+            put(src.at[line_rows(q), own], buf.at[pl.ds(brow0 + slot * 256, 256), right], 1, device)
 
     def plane_out():
         arrived(line_buf, 1)
@@ -104,14 +138,8 @@
             total += buf[brow0 + i * 256:brow0 + (i + 1) * 256, half:].astype(F32)
         src[line_rows(quarter), own] = total.astype(BF)
 
-        @pl.loop(1, 16)
-        def _(step):
-            device, r = relative(axis, step)
-            put(
-                src.at[plane_rows(r), own],
-                buf.at[pl.ds(pl.multiple_of(brow0 + 752 + step * 16, 16), 16), right],
-                2, device,
-            )
+        for device, r, slot in plane:
+            put(src.at[plane_rows(r), own], buf.at[pl.ds(brow0 + 768 + slot * 16, 16), right], 2, device)
 
     def plane_back():
         arrived(plane_buf, 2)
@@ -119,17 +147,15 @@
         total = src[plane_rows(rank), own].astype(F32) + jnp.sum(parts, axis=0)
         dst[plane_rows(rank), own] = total.astype(BF)
 
-        @pl.loop(1, 16)
-        def _(step):
-            device, _ = relative(axis, step)
-            piece = dst.at[plane_rows(rank), own]
+        piece = dst.at[plane_rows(rank), own]
+        for device, _, _ in plane:
             put(piece, piece, 3, device)
 
     def line_back():
         arrived(plane_buf, 3)
         piece = dst.at[line_rows(quarter), own]
-        for dq in (1, 3, 2):
-            put(piece, piece, 4, relative(axis, dq)[0])
+        for device, _, _ in line:
+            put(piece, piece, 4, device)
 
     def pair_back():
         arrived(line_buf, 4)
@@ -182,9 +208,7 @@
     for load in loads:
         load.start()
 
-    @pl.loop(1, DEV)
-    def _(step):
-        pl.semaphore_signal(barrier, inc=1, device_id=peer_of(step), device_id_type=MESH)
+    for_peers(lambda peer: pl.semaphore_signal(barrier, inc=1, device_id=peer, device_id_type=MESH))
 
     def block(device):
         return pl.ds(pl.multiple_of(device * CAP, CAP), CAP)
@@ -192,14 +216,14 @@
     def send(phase, c, src, dst):
         pltpu.make_async_copy(src.at[c, block(me)], dst.at[c, block(me)], recv_sem.at[phase, c]).start()
 
-        @pl.loop(1, DEV)
-        def _(step):
-            pin, board = peer_of(step)
+        def put(peer):
             pltpu.make_async_remote_copy(
-                src.at[c, block(pin * 4 + board)], dst.at[c, block(me)],
+                src.at[c, block(peer[0] * 4 + peer[1])], dst.at[c, block(me)],
                 send_sem.at[phase, c], recv_sem.at[phase, c],
-                device_id=(pin, board), device_id_type=MESH,
+                device_id=peer, device_id_type=MESH,
             ).start()
+
+        for_peers(put)
 
     def wait_sent(phase, c, src):
         part = src.at[c, pl.ds(0, (DEV - 1) * CAP)]
@@ -249,13 +273,13 @@
 
     pltpu.make_async_copy(idx_s.at[me], idx_r.at[me], idx_sem.at[1]).start()
 
-    @pl.loop(1, DEV)
-    def _(step):
-        pin, board = peer_of(step)
+    def put_table(peer):
         pltpu.make_async_remote_copy(
-            idx_s.at[pin * 4 + board], idx_r.at[me], idx_sem.at[0], idx_sem.at[1],
-            device_id=(pin, board), device_id_type=MESH,
+            idx_s.at[peer[0] * 4 + peer[1]], idx_r.at[me], idx_sem.at[0], idx_sem.at[1],
+            device_id=peer, device_id_type=MESH,
         ).start()
+
+    for_peers(put_table)
 
     @pl.loop(1, C)
     def _(c):
@@ -339,8 +363,8 @@
         wu[cols(n), :] = mm(nb_t[cols(n), :], feat[:, :H]).astype(BF)
 
     update_steps = [
-        grad_steps(wu, gu, 0, i, grad_buf.at[i // 2], (i % 2) * 1024, i % 3, gsend_sem.at[i], grecv_sem.at[i])
-        for i in range(4)
+        grad_steps(wu, gu, 0, i, grad_buf.at[i // 2], (i % 2) * 1024, axis, gsend_sem.at[i], grecv_sem.at[i])
+        for i, axis in enumerate((2, 0, 2, 1))
     ]
     for steps in update_steps:
         steps[0]()
@@ -367,8 +391,6 @@
             s1[c, tile(i)] = (walk_col[tile(i), :] * rows).astype(BF)
 
         send(3, c, s1, rb)
-        for steps in update_steps:
-            steps[1 + c]()
 
     message_steps = []
     for c in range(C):
@@ -387,14 +409,16 @@
             )
             for h in range(2)
         ])
-        if c < 2:
-            for steps in update_steps:
-                steps[5 + c]()
+        for steps in update_steps:
+            steps[1 + c]()
         for back in range(c + 1):
             for steps in message_steps[c - back]:
                 steps[back]()
 
     for tick in range(1, 7):
+        if tick < 3:
+            for steps in update_steps:
+                steps[4 + tick]()
         for back in range(tick, min(tick + C, 7)):
             for steps in message_steps[C - 1 + tick - back]:
                 steps[back]()
@@ -415,9 +439,9 @@
     output, gm, gu = pl.pallas_call(
         main_kernel,
         out_shape=(
-            jax.ShapeDtypeStruct((PINS, H), BF),
-            jax.ShapeDtypeStruct((F, H), BF),
-            jax.ShapeDtypeStruct((H, H), BF),
+            pltpu.VMEM((PINS, H), BF),
+            pltpu.VMEM((F, H), BF),
+            pltpu.VMEM((H, H), BF),
         ),
         in_specs=[hbm] * 4 + [vmem] * 4,
         out_specs=(vmem, vmem, vmem),
@@ -437,7 +461,7 @@
         ],
         name="layer",
         compiler_params=pltpu.CompilerParams(
-            collective_id=0, has_side_effects=True, vmem_limit_bytes=62 * 1024 * 1024
+            collective_id=0, has_side_effects=True, vmem_limit_bytes=54 * 1024 * 1024
         ),
     )(
         features, w_message, w_update, cotangent,

time: 281 us -> 261 us (0.929)
  Pallas kernels: 272 us -> 256 us
  local copies, waits for them, and re-layouts: 8.37 us -> 4.3 us
    pallas_call x1, Pallas kernels: 272 us -> 256 us  [body(): pl.pallas_call(main_kernel, out_shape=(pltpu.VMEM((PINS, H), BF), pltpu.V...]
    unnamed x5 -> x3, local copies, waits for them, and re-layouts: 8.37 us -> 4.3 us
where the time goes in v4:
time: 261 us
  Pallas kernels  256 us (98%)
  local copies, waits for them, and re-layouts  4.3 us (2%)
    pallas_call x1, Pallas kernels, body(): pl.pallas_call(main_kernel, out_shape=(pltpu.VMEM((PINS, H), BF), pltpu.V...  256 us

profile of v4, /device:TPU:1, one launch (start us, length us, event | category | flops | bytes accessed | tf_op | source)
XLA Modules:
  0.0 261.0 jit_solution(12228684490109747850)
XLA Ops:
  0.6 256.0 %layer.1 = (bf16[512,1024]{1,0:T(8,128)(2,1)S(1)}, bf16[2048,1024]{1,0:T(8,128)(2,1)S(1)}, bf16[1024,1024]{1,0:T(8,128)(2,1)S(1)}) custom-call(bf16[512,2048]{1,0:T(8,128)(2,1)} %feat_hbm.1, bf16[2048,1024]{1,0:T(8,128)(2,1)} %wm_hbm.1, bf16[1024,1024]{1,0:T(8,128)(2,1)} %wu_hbm.1, bf16[512,1024]{1,0:T(8,128)(2,1)} %cot_hbm.1, s32[16,128]{1,0:T(8,128)} %bitcast.9, ...), custom_call_target="tpu_custom_call" | custom-call | tf_op jit(solution)/shard_map/layer/pallas_call | solution.py:439
  256.7 1.0 copy.14
  257.6 1.3 copy.16
  259.0 2.0 copy.15

commit v5 on v4

--- a/solution.py
+++ b/solution.py
@@ -18,6 +18,24 @@
 W = 256
 C = H // W
 TILE = 512
+
+PLAN = (
+    (
+        (1, 0),
+    ),
+    (
+        (2, 0), (0, 1),
+    ),
+    (
+        (3, 0), (1, 1),
+    ),
+    (
+        (4, 0), (2, 1), (3, 1), (4, 1), (0, 2), (1, 2), (2, 2), (3, 2),
+        (4, 2), (0, 3), (1, 3), (2, 3), (3, 3), (4, 3), (0, 4), (1, 4),
+        (2, 4), (3, 4), (4, 4), (0, 5), (1, 5), (2, 5), (3, 5), (4, 5),
+        (0, 6), (1, 6), (2, 6), (3, 6), (4, 6),
+    ),
+)
 
 
 def silu_slope(value):
@@ -409,19 +427,10 @@
             )
             for h in range(2)
         ])
-        for steps in update_steps:
-            steps[1 + c]()
-        for back in range(c + 1):
-            for steps in message_steps[c - back]:
-                steps[back]()
-
-    for tick in range(1, 7):
-        if tick < 3:
-            for steps in update_steps:
-                steps[4 + tick]()
-        for back in range(tick, min(tick + C, 7)):
-            for steps in message_steps[C - 1 + tick - back]:
-                steps[back]()
+        blocks = [update_steps] + message_steps
+        for block_set, step in PLAN[c]:
+            for steps in blocks[block_set]:
+                steps[step]()
 
     @pl.loop(0, C)
     def _(c):

time: 261 us -> 248 us (0.950)
  Pallas kernels: 256 us -> 243 us
    pallas_call x1, Pallas kernels: 256 us -> 243 us  [body(): pl.pallas_call(main_kernel, out_shape=(pltpu.VMEM((PINS, H), BF), pltpu.V...]
where the time goes in v5:
time: 248 us
  Pallas kernels  243 us (98%)
  local copies, waits for them, and re-layouts  4.3 us (2%)
    pallas_call x1, Pallas kernels, body(): pl.pallas_call(main_kernel, out_shape=(pltpu.VMEM((PINS, H), BF), pltpu.V...  243 us

profile of v5, /device:TPU:1, one launch (start us, length us, event | category | flops | bytes accessed | tf_op | source)
XLA Modules:
  0.0 247.7 jit_solution(11273691456736502111)
XLA Ops:
  0.6 242.8 %layer.1 = (bf16[512,1024]{1,0:T(8,128)(2,1)S(1)}, bf16[2048,1024]{1,0:T(8,128)(2,1)S(1)}, bf16[1024,1024]{1,0:T(8,128)(2,1)S(1)}) custom-call(bf16[512,2048]{1,0:T(8,128)(2,1)} %feat_hbm.1, bf16[2048,1024]{1,0:T(8,128)(2,1)} %wm_hbm.1, bf16[1024,1024]{1,0:T(8,128)(2,1)} %wu_hbm.1, bf16[512,1024]{1,0:T(8,128)(2,1)} %cot_hbm.1, s32[16,128]{1,0:T(8,128)} %bitcast.9, ...), custom_call_target="tpu_custom_call" | custom-call | tf_op jit(solution)/shard_map/layer/pallas_call | solution.py:448
  243.4 1.0 copy.14
  244.4 1.3 copy.16
  245.7 2.0 copy.15

commit v6 on v5

--- a/solution.py
+++ b/solution.py
@@ -226,7 +226,10 @@
     for load in loads:
         load.start()
 
-    for_peers(lambda peer: pl.semaphore_signal(barrier, inc=1, device_id=peer, device_id_type=MESH))
+    zs, xs, core, ys = places()
+    for i in range(1, DEV):
+        peer = (zs[i // 32] + xs[i // 8 % 4] + (core if i % 8 < 4 else 1 - core), ys[i % 4])
+        pl.semaphore_signal(barrier, inc=1, device_id=peer, device_id_type=MESH)
 
     def block(device):
         return pl.ds(pl.multiple_of(device * CAP, CAP), CAP)
@@ -281,6 +284,8 @@
     project(0)
     pl.semaphore_wait(barrier, DEV - 1)
     send(0, 0, s0, ra)
+    project(1)
+    send(0, 1, s0, ra)
 
     table[:CAP, :] = (walks * 256 + sboard_ref[...]).astype(F32)
     table[...] = table[...].T
@@ -299,10 +304,39 @@
 
     for_peers(put_table)
 
-    @pl.loop(1, C)
+    @pl.loop(2, C)
     def _(c):
         project(c)
         send(0, c, s0, ra)
+
+    pltpu.make_async_copy(idx_r, idx_r, idx_sem.at[1]).wait()
+    sent_idx = idx_s.at[pl.ds(0, DEV - 1)]
+    pltpu.make_async_copy(sent_idx, sent_idx, idx_sem.at[0]).wait()
+
+    @pl.loop(0, DEV)
+    def _(row):
+        table[pl.ds(row, 1), :] = idx_r[row].astype(F32)
+
+    received = table[...].astype(jnp.int32)
+    brd_tab = (received % 256).astype(F32)
+    bwalk_tab = (received // 256).astype(F32)
+    brd_t[...] = (iota((SLOTS, BOARDS), 1).astype(F32) == to_column(brd_tab)).astype(F32).astype(BF)
+    walk_col[...] = to_column(bwalk_tab)
+    match = iota((BOARDS, SLOTS), 0).astype(F32) == to_row(brd_tab)
+    weights = jnp.where(match, to_row(bwalk_tab), 0.0)
+    brd_w[...] = weights.astype(BF)
+    bdeg[...] = jnp.maximum(jnp.sum(weights, axis=1, keepdims=True), 1.0)
+
+    @pl.loop(0, C)
+    def _(c):
+        wait_received(0, c, ra)
+        brow_buf[0] = (mm(brd_w[...], ra[c]) / bdeg[...]).astype(BF)
+
+        @pl.loop(0, SLOTS // TILE)
+        def _(i):
+            s1[c, tile(i)] = mm(brd_t[tile(i), :], brow_buf[0]).astype(BF)
+
+        send(1, c, s1, rb)
 
     pin_row = to_row(pin_hi) * 256.0 + to_row(pin_lo)
     walk_row = to_row(walk_tab)
@@ -316,35 +350,6 @@
     scale_col[...] = own_walk / jnp.maximum(slot_degree, 1.0)
     feat_t[...] = feat[...].T
 
-    pltpu.make_async_copy(idx_r, idx_r, idx_sem.at[1]).wait()
-    sent_idx = idx_s.at[pl.ds(0, DEV - 1)]
-    pltpu.make_async_copy(sent_idx, sent_idx, idx_sem.at[0]).wait()
-
-    @pl.loop(0, DEV)
-    def _(row):
-        table[pl.ds(row, 1), :] = idx_r[row].astype(F32)
-
-    received = table[...].astype(jnp.int32)
-    brd_tab = (received % 256).astype(F32)
-    bwalk_tab = (received // 256).astype(F32)
-    brd_t[...] = (iota((SLOTS, BOARDS), 1).astype(F32) == to_column(brd_tab)).astype(F32).astype(BF)
-    walk_col[...] = to_column(bwalk_tab)
-    match = iota((BOARDS, SLOTS), 0).astype(F32) == to_row(brd_tab)
-    weights = jnp.where(match, to_row(bwalk_tab), 0.0)
-    brd_w[...] = weights.astype(BF)
-    bdeg[...] = jnp.maximum(jnp.sum(weights, axis=1, keepdims=True), 1.0)
-
-    @pl.loop(0, C)
-    def _(c):
-        wait_received(0, c, ra)
-        brow_buf[0] = (mm(brd_w[...], ra[c]) / bdeg[...]).astype(BF)
-
-        @pl.loop(0, SLOTS // TILE)
-        def _(i):
-            s1[c, tile(i)] = mm(brd_t[tile(i), :], brow_buf[0]).astype(BF)
-
-        send(1, c, s1, rb)
-
     brd_w[...] = (brd_w[...].astype(F32) > 0.0).astype(F32).astype(BF)
     loads[2].wait()
     loads[3].wait()
@@ -439,6 +444,28 @@
 
     for steps in update_steps + message_steps[0] + message_steps[1] + message_steps[2] + message_steps[3]:
         steps[7]()
+
+
+def store_kernel(a, b, c, x, y, z, sems):
+    copies = [pltpu.make_async_copy(s, d, sems.at[i]) for i, (s, d) in enumerate(((a, x), (b, y), (c, z)))]
+    for copy in copies:
+        copy.start()
+    for copy in copies:
+        copy.wait()
+
+
+def finish_results(*results):
+    vmem = pl.BlockSpec(memory_space=pltpu.VMEM)
+    hbm = pl.BlockSpec(memory_space=pl.ANY)
+    return pl.pallas_call(
+        store_kernel,
+        out_shape=tuple(pltpu.HBM(r.shape, r.dtype) for r in results),
+        in_specs=[vmem] * 3,
+        out_specs=(hbm,) * 3,
+        scratch_shapes=[pltpu.SemaphoreType.DMA((3,))],
+        name="store",
+        compiler_params=pltpu.CompilerParams(vmem_limit_bytes=8 * 1024 * 1024),
+    )(*results)
 
 
 def body(features, w_message, w_update, cotangent, slot_pin, slot_board, slot_walk, pair_count):
@@ -476,7 +503,7 @@
         features, w_message, w_update, cotangent,
         slot_pin[0].T, slot_board[0].T, slot_walk[0].T, pair_count,
     )
-    return output, gm, gu
+    return finish_results(output, gm, gu)
 
 
 def solution(mesh):

time: 248 us -> 247 us (level)
  local copies, waits for them, and re-layouts: 4.3 us -> 0 us
  Pallas kernels: 243 us -> 246 us
    unnamed x3 -> x0, local copies, waits for them, and re-layouts: 4.3 us -> none
    pallas_call x0 -> x1, Pallas kernels: none -> 3.07 us  [finish_results(): pl.pallas_call(store_kernel, out_shape=tuple((pltpu.HBM(r.shape, r.dtype)...]
where the time goes in v6:
time: 247 us
  Pallas kernels  246 us (100%)
    pallas_call x1, Pallas kernels, body(): pl.pallas_call(main_kernel, out_shape=(pltpu.VMEM((PINS, H), BF), pltpu.V...  243 us

profile of v6, /device:TPU:1, one launch (start us, length us, event | category | flops | bytes accessed | tf_op | source)
XLA Modules:
  0.0 246.6 jit_solution(15721926129952593965)
XLA Ops:
  0.6 242.7 %layer.1 = (bf16[512,1024]{1,0:T(8,128)(2,1)S(1)}, bf16[2048,1024]{1,0:T(8,128)(2,1)S(1)}, bf16[1024,1024]{1,0:T(8,128)(2,1)S(1)}) custom-call(bf16[512,2048]{1,0:T(8,128)(2,1)} %feat_hbm.1, bf16[2048,1024]{1,0:T(8,128)(2,1)} %wm_hbm.1, bf16[1024,1024]{1,0:T(8,128)(2,1)} %wu_hbm.1, bf16[512,1024]{1,0:T(8,128)(2,1)} %cot_hbm.1, s32[16,128]{1,0:T(8,128)} %bitcast.9, ...), custom_call_target="tpu_custom_call" | custom-call | tf_op jit(solution)/shard_map/layer/pallas_call | solution.py:475
  243.4 3.1 %store.1 = (bf16[512,1024]{1,0:T(8,128)(2,1)}, bf16[2048,1024]{1,0:T(8,128)(2,1)}, bf16[1024,1024]{1,0:T(8,128)(2,1)}) custom-call(bf16[512,1024]{1,0:T(8,128)(2,1)S(1)} %get-tuple-element.6.a, bf16[2048,1024]{1,0:T(8,128)(2,1)S(1)} %get-tuple-element.7.b, bf16[1024,1024]{1,0:T(8,128)(2,1)S(1)} %get-tuple-element.8.c), custom_call_target="tpu_custom_call" | custom-call | tf_op jit(solution)/shard_map/store/pallas_call | solution.py:460
